TPU v7x, 128 devices: a whole 4x4x4 slice. The times are simulated.
128 devices in a mesh: uv: 16 (over x, y), chan: 8 (over z, core).
Axes of the slice: x: 4, y: 4, z: 4, core: 2. Of those that a mesh axis runs over, the one named last changes fastest.
Arguments:
- vis: bfloat16 [196608, 2, 1024], P('uv', None, 'chan'), may hold values from -6 to 6
- row_cell: int32 [196608], P('uv'), may hold values from 0 to 127
- tap_weight: bfloat16 [8, 196608], P(None, 'uv'), may hold values from 0.029907227 to 0.29882812
- tap_offset: int32 [8], replicated, may hold values from -32 to 32
- block_tile: int32 [1536], P('uv'), may hold values from 0 to 159, as said below
- tile_owner: int32 [160], replicated, may hold values from 0 to 15, as said below
- galaxy: bfloat16 [304, 128, 2048], P('uv', 'chan'), may hold values from -6 to 6
Outputs:
- delay_cube: bfloat16 [304, 128, 2048], P('uv', 'chan')
- cross_power: float32 [304, 1024], P('uv')
Inputs may be any that keep to these rules, and one draw needn't show every extreme that they name: `tile_owner`: each of the 16 owners holds 1 to 19 tiles, and some owner exactly 19. `block_tile`: of the 96 row blocks of one index of uv, at most 11 lie in tiles of one owner, and exactly 11 lie in the tiles of some owner.
All inputs are finite; a program needn't handle non-finite values.
Results may differ from a plain program's by a relative error of at most 0.0059.
Values may be sent and summed in bfloat16 or wider, within the bound.
A program may use at most 128 MiB of HBM per device.

v0:
```python
import math

import jax
import jax.numpy as jnp
from jax import lax
from jax.sharding import PartitionSpec as P

CH = 1024
BR = 128
TC = 128
KT = 8
TILES_DEV = 10


def from_everyone(x, axis):
    size = lax.axis_size(axis)
    return lax.all_to_all(jnp.broadcast_to(x[None], (size, *x.shape)), axis, 0, 0, tiled=True)


def over_copies(x, axis):
    return from_everyone(x, axis).sum(axis=0)


def tile_ranks(tile_owner, owners):
    onehot = (tile_owner[:, None] == jnp.arange(owners, dtype=jnp.int32)[None, :]).astype(jnp.int32)
    before = jnp.cumsum(onehot, axis=0) - onehot
    return jnp.sum(before * onehot, axis=1)


def kernel_matrix(cells, weights, tap_offset):
    positions = jnp.arange(TC, dtype=jnp.int32)
    total = jnp.zeros(cells.shape[:-1] + (TC, cells.shape[-1]), jnp.float32)
    for k in range(KT):
        target = cells + tap_offset[k]
        hit = target[..., None, :] == positions[:, None]
        total = total + jnp.where(
            hit, weights[..., k, :].astype(jnp.float32)[..., None, :], jnp.float32(0.0)
        )
    return total.astype(jnp.bfloat16)


def delay_table():
    freq = jnp.arange(CH, dtype=jnp.int32)
    phase = (freq[:, None] * freq[None, :] % CH).astype(jnp.float32) * jnp.float32(
        2.0 * math.pi / CH
    )
    cosine = jnp.cos(phase)
    sine = jnp.sin(phase)
    x = freq.astype(jnp.float32) * jnp.float32(2.0 * math.pi / CH)
    taper = 0.35875 - 0.48829 * jnp.cos(x) + 0.14128 * jnp.cos(2.0 * x) - 0.01168 * jnp.cos(3.0 * x)
    scale = (taper / jnp.float32(math.sqrt(CH)))[:, None]
    upper = jnp.concatenate([cosine * scale, -sine * scale], axis=1)
    lower = jnp.concatenate([sine * scale, cosine * scale], axis=1)
    return jnp.concatenate([upper, lower], axis=0).astype(jnp.bfloat16)


def body(vis, row_cell, tap_weight, tap_offset, block_tile, tile_owner, galaxy):
    n_owners = lax.axis_size("uv")
    nblocks = block_tile.shape[0]
    mean_load = nblocks // n_owners
    capacity = mean_load + (TILES_DEV - 1) * mean_load // TILES_DEV
    slots_dev = 2 * TILES_DEV - 1
    chan_dev = vis.shape[2]
    buffer_size = n_owners * capacity
    rank_of_tile = tile_ranks(tile_owner, n_owners)
    target_owner = tile_owner[block_tile]
    owner_hot = (target_owner[:, None] == jnp.arange(n_owners, dtype=jnp.int32)[None, :]).astype(
        jnp.int32
    )
    earlier = jnp.cumsum(owner_hot, axis=0) - owner_hot
    place = target_owner * capacity + jnp.sum(earlier * owner_hot, axis=1)
    blocks = vis.reshape(nblocks, BR, 2 * chan_dev)
    cells = row_cell.reshape(nblocks, BR)
    weights = jnp.transpose(tap_weight.reshape(KT, nblocks, BR), (1, 0, 2))
    sent_vis = jnp.zeros((buffer_size, BR, 2 * chan_dev), jnp.bfloat16).at[place].set(blocks)
    sent_tile = jnp.full((buffer_size,), -1, jnp.int32).at[place].set(block_tile)
    sent_cells = jnp.zeros((buffer_size, BR), jnp.int32).at[place].set(cells)
    sent_weights = jnp.zeros((buffer_size, KT, BR), jnp.bfloat16).at[place].set(weights)
    got_vis, got_tile, got_cells, got_weights = (
        lax.all_to_all(sent_vis, "uv", split_axis=0, concat_axis=0, tiled=True),
        lax.all_to_all(sent_tile, "uv", split_axis=0, concat_axis=0, tiled=True),
        lax.all_to_all(sent_cells, "uv", split_axis=0, concat_axis=0, tiled=True),
        lax.all_to_all(sent_weights, "uv", split_axis=0, concat_axis=0, tiled=True),
    )
    got_matrix = kernel_matrix(got_cells, got_weights, tap_offset)
    contrib = jnp.einsum("bcr,brf->bcf", got_matrix, got_vis, preferred_element_type=jnp.float32)
    slot = jnp.where(got_tile >= 0, rank_of_tile[jnp.maximum(got_tile, 0)], -1)
    pick = (slot[:, None] == jnp.arange(slots_dev, dtype=jnp.int32)[None, :]).astype(jnp.float32)
    grid = jnp.einsum("bs,bcf->scf", pick, contrib, precision=lax.Precision.HIGHEST)
    gridded = grid.astype(jnp.bfloat16).reshape(slots_dev, TC, 2, chan_dev)
    table = delay_table()
    piece = lax.all_to_all(gridded, "chan", split_axis=1, concat_axis=3, tiled=True)
    count = piece.shape[0]
    cells_part = piece.shape[1]
    flat = piece.reshape(count * cells_part, 2 * CH)
    out = jnp.dot(flat, table, preferred_element_type=jnp.float32)
    delay = out.reshape(count, cells_part, 2 * CH)
    galaxy_f = galaxy.astype(jnp.float32)
    product = delay[..., :CH] * galaxy_f[..., :CH] + delay[..., CH:] * galaxy_f[..., CH:]
    local_power = jnp.sum(product, axis=1)
    power = over_copies(local_power, "chan") / jnp.float32(math.sqrt(TC))
    return (delay.astype(jnp.bfloat16), power)


def solution(mesh):
    return jax.shard_map(
        body,
        mesh=mesh,
        in_specs=(
            P("uv", None, "chan"),
            P("uv"),
            P(None, "uv"),
            P(),
            P("uv"),
            P(),
            P("uv", "chan", None),
        ),
        out_specs=(P("uv", "chan", None), P("uv", None)),
        check_vma=False,
    )
```

profile of v0, /device:TPU:1, one launch (start us, length us, event | category | flops | bytes accessed | tf_op | source)
XLA Modules:
  0.0 373.8 jit_solution(15880393098052350849)
XLA Ops:
  0.6 0.0 copy-start
  0.6 0.7 compare_select_fusion.1
  1.3 1.6 gather_fusion
  3.0 0.1 fusion.41
  3.0 0.1 reduce_window_sum.26
  3.2 0.2 select_reduce_fusion
  3.4 1.0 scatter_custom_fusion
  4.4 0.7 all_to_all.32
  5.1 7.6 %all-to-all-start = ((s32[16,11,1]{1,2,0:T(1,128)}), s32[16,11,1]{1,2,0:T(1,128)S(1)}, u32[]{:S(2)}, u32[]{:S(2)}) async-start(s32[16,11,1]{1,2,0:T(1,128)} %bitcast.2), calls=%async_computation | async-start | bytes 16384 | tf_op jit(solution)/shard_map/all_to_all | solution.py:81
  12.7 0.8 scatter_custom_fusion.1
  13.5 0.6 all_to_all.34
  14.2 4.8 %all-to-all-done = s32[16,11,1]{1,2,0:T(1,128)S(1)} async-done(((s32[16,11,1]{1,2,0:T(1,128)}), s32[16,11,1]{1,2,0:T(1,128)S(1)}, u32[]{:S(2)}, u32[]{:S(2)}) %all-to-all-start) | async-done | bytes 736 | tf_op jit(solution)/shard_map/all_to_all | solution.py:81
  19.0 3.5 all-to-all-start.1
  22.5 0.8 broadcast_in_dim.150
  23.3 10.6 %scatter_fusion = bf16[176,8,128]{2,1,0:T(8,128)(2,1)} fusion(bf16[176,8,128]{2,1,0:T(8,128)(2,1)} %broadcast_in_dim.150, s32[96]{0:T(128)S(1)} %fusion.48, bf16[96,8,128]{2,1,0:T(8,128)(2,1)} %bitcast.57), kind=kCustom, calls=%fused_computation.4 | custom fusion | bytes 590208 | tf_op jit(solution)/shard_map/scatter | solution.py:78
  33.9 0.0 all-to-all-done.1
  33.9 6.6 %all-to-all-start.2 = ((bf16[176,8,128]{2,1,0:T(8,128)(2,1)}), bf16[176,8,128]{2,1,0:T(8,128)(2,1)S(1)}, u32[]{:S(2)}, u32[]{:S(2)}) async-start(bf16[176,8,128]{2,1,0:T(8,128)(2,1)} %scatter_fusion), calls=%async_computation.2 | async-start | bytes 720896 | tf_op jit(solution)/shard_map/all_to_all | solution.py:83
  40.5 10.8 %reshape.219 = bf16[96,128,256]{2,1,0:T(8,128)(2,1)} reshape(bf16[12288,2,128]{2,1,0:T(2,128)(2,1)} %param.7) | data formatting | bytes 12582912 | tf_op jit(solution)/shard_map/reshape | solution.py:72
  51.3 5.8 %broadcast_in_dim.176 = bf16[176,128,256]{2,1,0:T(8,128)(2,1)} broadcast(bf16[]{:T(256)} %constant.28.clone.1), dimensions={} | broadcast | bytes 11534338 | tf_op jit(solution)/shard_map/broadcast_in_dim | solution.py:75
  57.1 17.7 %scatter_fusion.1 = bf16[176,128,256]{2,1,0:T(8,128)(2,1)} fusion(bf16[176,128,256]{2,1,0:T(8,128)(2,1)} %broadcast_in_dim.176, s32[96]{0:T(128)S(1)} %fusion.48, bf16[96,128,256]{2,1,0:T(8,128)(2,1)} %reshape.219), kind=kCustom, calls=%fused_computation.5 | custom fusion | bytes 18874752 | tf_op jit(solution)/shard_map/scatter | solution.py:75
  74.8 0.0 all-to-all-done.2
  74.8 6.9 %all-to-all-start.3 = ((bf16[176,128,256]{2,1,0:T(8,128)(2,1)}), bf16[176,128,256]{2,1,0:T(8,128)(2,1)}, u32[]{:S(2)}, u32[]{:S(2)}) async-start(bf16[176,128,256]{2,1,0:T(8,128)(2,1)} %scatter_fusion.1), calls=%async_computation.3 | async-start | bytes 23068672 | tf_op jit(solution)/shard_map/all_to_all | solution.py:80
  81.8 0.6 reduce-window.6
  82.3 0.2 slice_reduce_fusion
  82.6 0.7 fusion.53
  83.2 0.1 bitcast_bitcast_fusion
  83.4 0.1 reshape.185
  83.5 0.1 ge.11
  83.6 1.6 gather_fusion.1
  85.3 5.1 %broadcast_add_fusion.7 = (s32[16,11,128]{2,1,0:T(8,128)S(1)}, s32[16,11,128]{2,1,0:T(8,128)S(1)}, s32[16,11,128]{2,1,0:T(8,128)S(1)}, s32[16,11,128]{2,1,0:T(8,...) fusion(s32[16,11,128]{2,1,0:T(8,128)S(1)} %all-to-all-done.1, ...), kind=kLoop, calls=%fused_computation.76 | loop fusion | flops 180224 | bytes 811040 | tf_op jit(solution)/shard_map/add | solution.py:34
  90.5 0.5 slice_convert_fusion.7
  91.0 169.2 %all-to-all-done.3 = bf16[176,128,256]{2,1,0:T(8,128)(2,1)} async-done(((bf16[176,128,256]{2,1,0:T(8,128)(2,1)}), bf16[176,128,256]{2,1,0:T(8,128)(2,1)}, u32[]{:S(2)}, u32[]{:S(2)}) %all-to-all-start.3) | async-done | bytes 11534368 | tf_op jit(solution)/shard_map/all_to_all | solution.py:80
  260.2 17.7 %fusion.9 = f32[176,128,256]{2,1,0:T(8,128)} fusion(bf16[176,128,256]{2,1,0:T(8,128)(2,1)} %all-to-all-done.3, f32[176,128]{1,0:T(8,128)S(1)} %bitcast.59, s32[176,128]{1,0:T(8,128)S(1)} %add.221, f32[176,128]{1,0:T(8,128)S(1)} %bitcast.60, s32[176,128]{1,0:T(8,128)S(1)} %add.217, f32[176,128]{1,0:T(8,128)S(1)} %bitcast.61, s32[176,128]{1,0:T(8,128)S(1)} %add.213, ...), kind=kOutput, calls=%fused_computation.28 | convolution fusion | flops 1545601024 | bytes 36044800 | tf_op jit(solution)/shard_map/bcr,brf->bcf/dot_general | solution.py:86
  277.9 26.9 %fusion.34 = bf16[19,128,256]{2,0,1:T(8,128)(2,1)S(1)} fusion(f32[176,128,256]{2,1,0:T(8,128)} %fusion.9, s32[176]{0:T(256)S(1)} %broadcast_select_fusion), kind=kOutput, calls=%fused_computation.56 | convolution fusion | flops 1315540224 | bytes 24314560 | tf_op jit(solution)/shard_map/bs,bcf->scf/dot_general | solution.py:89
  304.8 1.4 copy.40
  306.2 2.8 copy.41
  309.0 12.0 %all-to-all-start.4 = ((bf16[19,128,2,128]{3,2,0,1:T(2,128)(2,1)}), bf16[19,128,2,128]{3,2,0,1:T(2,128)(2,1)}, u32[]{:S(2)}, u32[]{:S(2)}) async-start(bf16[19,128,2,128]{3,2,0,1:T(2,128)(2,1)} %copy.41), calls=%async_computation.4 | async-start | bytes 2490368 | tf_op jit(solution)/shard_map/all_to_all | solution.py:92
  321.0 1.6 convert_element_type.66
  322.6 0.1 subtract_multiply_fusion
  322.6 19.1 %multiply_convert_fusion.1 = (bf16[1024,1024]{1,0:T(8,128)(2,1)}, bf16[1024,1024]{1,0:T(8,128)(2,1)}, bf16[1024,1024]{1,0:T(8,128)(2,1)}) fusion(f32[1024]{0:T(1024)S(1)} %subtract_multiply_fusion), kind=kLoop, calls=%fused_computation.50 | loop fusion | flops 22020096 | bytes 6295552 | tf_op jit(solution)/shard_map/convert.16
  341.7 1.6 copy.42
  343.3 1.4 copy.43
  344.7 3.2 dot_general.13
  347.9 7.6 %fusion.54 = (bf16[19,16,2048]{2,1,0:T(8,128)(2,1)}, f32[19,16,2048]{2,1,0:T(8,128)S(1)}) fusion(bf16[19,16,2048]{2,1,0:T(8,128)(2,1)} %dot_general.13, bf16[1024,1024]{1,0:T(8,128)(2,1)} %get-tuple-element.20, bf16[1024,1024]{1,0:T(8,128)(2,1)} %get-tuple-element.19, bf16[1024,1024]{1,0:T(8,128)(2,1)} %get-tuple-element.18), kind=kOutput, calls=%fused_computation.111 | convolution fusion | flops 2584313856 | bytes 11272192 | tf_op jit(solution)/shard_map/dot_general | solution.py:96
  355.5 0.7 fusion.38
  356.2 0.1 broadcast_in_dim.177
  356.3 16.8 %all_to_all.48 = f32[8,19,1024]{2,1,0:T(8,128)S(1)} all-to-all(f32[8,19,1024]{2,1,0:T(8,128)S(1)} %broadcast_in_dim.177), channel_id=1, replica_groups=mesh['uv'=16,'chan'=8] {'chan'}, dimensions={0} | all-to-all | bytes 1245184 | tf_op jit(solution)/shard_map/all_to_all | solution.py:17
  373.2 0.7 broadcast_multiply_fusion
  (28 shorter events, 0.3 us)
Async XLA Ops:
  0.6 12.0 %copy-start = (s32[12288]{0:T(1024)S(1)}, s32[12288]{0:T(1024)}, u32[]{:S(2)}) copy-start(s32[12288]{0:T(1024)} %param.8) | copy-start | bytes 147460
  5.1 13.9 %all-to-all-start = ((s32[16,11,1]{1,2,0:T(1,128)}), s32[16,11,1]{1,2,0:T(1,128)S(1)}, u32[]{:S(2)}, u32[]{:S(2)}) async-start(s32[16,11,1]{1,2,0:T(1,128)} %bitcast.2), calls=%async_computation | async-start | bytes 16384 | tf_op jit(solution)/shard_map/all_to_all | solution.py:81
  19.0 14.9 %all-to-all-start.1 = ((s32[16,11,128]{2,1,0:T(8,128)}), s32[16,11,128]{2,1,0:T(8,128)S(1)}, u32[]{:S(2)}, u32[]{:S(2)}) async-start(s32[16,11,128]{2,1,0:T(8,128)} %all_to_all.34), calls=%async_computation.1 | async-start | bytes 262144 | tf_op jit(solution)/shard_map/all_to_all | solution.py:82
  33.9 40.9 %all-to-all-start.2 = ((bf16[176,8,128]{2,1,0:T(8,128)(2,1)}), bf16[176,8,128]{2,1,0:T(8,128)(2,1)S(1)}, u32[]{:S(2)}, u32[]{:S(2)}) async-start(bf16[176,8,128]{2,1,0:T(8,128)(2,1)} %scatter_fusion), calls=%async_computation.2 | async-start | bytes 720896 | tf_op jit(solution)/shard_map/all_to_all | solution.py:83
  74.8 6.9 %copy-start.2 = (s32[160]{0:T(256)S(1)}, s32[160]{0:T(256)}, u32[]{:S(2)}) copy-start(s32[160]{0:T(256)} %param.12) | copy-start | bytes 1924
  74.8 7.7 %copy-start.3 = (s32[8]{0:T(128)S(1)}, s32[8]{0:T(128)}, u32[]{:S(2)}) copy-start(s32[8]{0:T(128)} %param.10) | copy-start | bytes 100
  74.8 185.3 %all-to-all-start.3 = ((bf16[176,128,256]{2,1,0:T(8,128)(2,1)}), bf16[176,128,256]{2,1,0:T(8,128)(2,1)}, u32[]{:S(2)}, u32[]{:S(2)}) async-start(bf16[176,128,256]{2,1,0:T(8,128)(2,1)} %scatter_fusion.1), calls=%async_computation.3 | async-start | bytes 23068672 | tf_op jit(solution)/shard_map/all_to_all | solution.py:80
  309.0 32.7 %all-to-all-start.4 = ((bf16[19,128,2,128]{3,2,0,1:T(2,128)(2,1)}), bf16[19,128,2,128]{3,2,0,1:T(2,128)(2,1)}, u32[]{:S(2)}, u32[]{:S(2)}) async-start(bf16[19,128,2,128]{3,2,0,1:T(2,128)(2,1)} %copy.41), calls=%async_computation.4 | async-start | bytes 2490368 | tf_op jit(solution)/shard_map/all_to_all | solution.py:92
  347.9 25.9 %copy-start.1 = (s32[12288]{0:T(1024)S(1)}, s32[12288]{0:T(1024)}, u32[]{:S(2)}) copy-start(s32[12288]{0:T(1024)} %param.8) | copy-start | bytes 147460
where the time goes:
time: 379 us; the launch traced here: 374 us
  waiting for transfers between devices  174 us (46%)
  local copies, waits for them, and re-layouts  63.7 us (17%)
  matrix products  52.2 us (14%)
  starting transfers between devices  36.5 us (10%)
  other arithmetic  29.6 us (8%)
  blocking collectives  16.8 us (4%)
    all_to_all x1, waiting for transfers between devices, body(): lax.all_to_all(sent_vis, 'uv', split_axis=0, concat_axis=0, tiled=True)  169 us
    dot_general x1, matrix products, body(): jnp.einsum('bs,bcf->scf', pick, contrib, precision=lax.Precision.HIGHEST)  26.9 us
    another operation x5, other arithmetic  19.8 us
    dot_general x1, matrix products, body(): jnp.einsum('bcr,brf->bcf', got_matrix, got_vis, preferred_element_type=jn...  17.7 us
    scatter x1, local copies, waits for them, and re-layouts, body(): jnp.zeros((buffer_size, BR, 2 * chan_dev), jnp.bfloat16).at[place]  17.7 us
    all_to_all x1, blocking collectives, from_everyone(): lax.all_to_all(jnp.broadcast_to(x[None], (size, *x.shape)), axis, 0, 0, t...  16.8 us
    all_to_all x1, starting transfers between devices, body(): lax.all_to_all(gridded, 'chan', split_axis=1, concat_axis=3, tiled=True)  12 us
    reshape x1, local copies, waits for them, and re-layouts, body(): blocks = vis.reshape(nblocks, BR, 2 * chan_dev)  10.8 us
  transfers between devices with their start and end apart: 5, of which 2 were waited for; matrix products, arithmetic and copies ran while one was open for 20% of the time, Pallas kernels for 0%

commit v1 on v0

v1 whole, which is shorter than its diff:
```python
import functools
import math

import jax
import jax.numpy as jnp
import numpy as np
from jax import lax
from jax.experimental import pallas as pl
from jax.experimental.pallas import tpu as pltpu
from jax.sharding import PartitionSpec as P

MESH = pl.DeviceIdType.MESH
CH = 1024
BR = 128
TC = 128
KT = 8
N_OWN = 16
CAP = 11
SLOTS = 19
SIDE = 4
F32 = jnp.float32
BF16 = jnp.bfloat16
MIB = 2**20


def table_constant(n_chan):
    freq = np.arange(CH, dtype=np.int64)
    phase = ((freq[:, None] * freq[None, :]) % CH).astype(np.float32) * np.float32(2.0 * math.pi / CH)
    cosine, sine = np.cos(phase), np.sin(phase)
    x = freq.astype(np.float32) * np.float32(2.0 * math.pi / CH)
    taper = (
        np.float32(0.35875)
        - np.float32(0.48829) * np.cos(x)
        + np.float32(0.14128) * np.cos(np.float32(2.0) * x)
        - np.float32(0.01168) * np.cos(np.float32(3.0) * x)
    )
    scale = (taper / np.float32(math.sqrt(CH)))[:, None]
    upper = np.concatenate([cosine * scale, -sine * scale], axis=1)
    lower = np.concatenate([sine * scale, cosine * scale], axis=1)
    table = np.stack([upper, lower]).reshape(2, n_chan, CH // n_chan, 2 * CH)
    return table.transpose(1, 0, 2, 3).reshape(2 * CH, 2 * CH).astype(jnp.bfloat16)


def split_constant():
    p = np.zeros((2 * BR, 2 * BR), np.float32)
    r = np.arange(BR)
    p[r, 2 * r] = 1.0
    p[BR + r, 2 * r + 1] = 1.0
    return p.astype(jnp.bfloat16)


def peer(uv, chan, dx=0, dy=0):
    x = lax.rem(uv // SIDE + dx, SIDE)
    y = lax.rem(lax.rem(uv, SIDE) + dy, SIDE)
    return (x * SIDE + y, chan)


def lists_kernel(block_tile, tile_owner, blk_ref, slot_ref, rank, count):
    def clear(o, _):
        count[o] = 0
        for i in range(CAP):
            blk_ref[o, i] = 0
            slot_ref[o, i] = SLOTS
        return 0

    lax.fori_loop(0, N_OWN, clear, 0)

    def tiles(t, _):
        o = tile_owner[t]
        rank[t] = count[o]
        count[o] = count[o] + 1
        return 0

    lax.fori_loop(0, tile_owner.shape[0], tiles, 0)
    for o in range(N_OWN):
        count[o] = 0

    def blocks(b, _):
        t = block_tile[b]
        o = tile_owner[t]
        i = count[o]
        blk_ref[o, i] = b
        slot_ref[o, i] = rank[t]
        count[o] = i + 1
        return 0

    lax.fori_loop(0, block_tile.shape[0], blocks, 0)


def block_lists(block_tile, tile_owner):
    smem = pl.BlockSpec(memory_space=pltpu.SMEM)
    table = jax.ShapeDtypeStruct((N_OWN, 128), jnp.int32)
    return pl.pallas_call(
        lists_kernel,
        out_shape=(table, table),
        in_specs=[smem, smem],
        out_specs=(smem, smem),
        scratch_shapes=[pltpu.SMEM(tile_owner.shape, jnp.int32), pltpu.SMEM((N_OWN,), jnp.int32)],
        name="block_lists",
    )(block_tile, tile_owner)


def grid_send_kernel(
    blk, slot_vm, vis, target, weight, split, rec, meta, send, send_sem, recv_sem, local_sem, msend, mrecv, mlocal
):
    uv, chan = lax.axis_index("uv"), lax.axis_index("chan")
    barrier = pltpu.get_barrier_semaphore()
    for d in range(1, SIDE):
        pl.semaphore_signal(barrier, inc=1, device_id=peer(uv, chan, dx=d), device_id_type=MESH)
        pl.semaphore_signal(barrier, inc=1, device_id=peer(uv, chan, dy=d), device_id_type=MESH)
    pl.semaphore_wait(barrier, 2 * (SIDE - 1))

    def meta_copy(h, d):
        k = h * SIDE + d
        if d == 0:
            return pltpu.make_async_copy(slot_vm, meta.at[k], mlocal.at[h])
        device = peer(uv, chan, dx=d) if h == 0 else peer(uv, chan, dy=d)
        return pltpu.make_async_remote_copy(
            slot_vm, meta.at[k], msend.at[k], mrecv.at[k], device_id=device, device_id_type=MESH
        )

    for h in range(2):
        for d in range(SIDE):
            meta_copy(h, d).start()

    cells = lax.broadcasted_iota(jnp.int32, (TC, BR), 0)

    def copy(h, dx, dy):
        q = dx * SIDE + dy
        out, src = (dy, dx) if h == 0 else (dx, dy)
        if src == 0:
            return pltpu.make_async_copy(send.at[h, q], rec.at[h, out, src], local_sem.at[h, out])
        device = peer(uv, chan, dx=dx) if h == 0 else peer(uv, chan, dy=dy)
        return pltpu.make_async_remote_copy(
            send.at[h, q],
            rec.at[h, out, src],
            send_sem.at[h, out, src],
            recv_sem.at[h, out, src],
            device_id=device,
            device_id_type=MESH,
        )

    order = sorted(((dx, dy) for dx in range(SIDE) for dy in range(SIDE)), key=lambda v: (min(v) == 0, v != (2, 2)))
    for dx, dy in order:
        q = dx * SIDE + dy
        owner, _ = peer(uv, chan, dx=dx, dy=dy)
        def one(i, _, q=q, owner=owner):
            b = blk[owner, i]
            t, w = target[b], weight[b]
            total = jnp.zeros((TC, BR), F32)
            for k in range(KT):
                total = total + jnp.where(t[k : k + 1, :] == cells, w[k : k + 1, :], 0.0)
            parts = jnp.dot(split[...], vis[b], preferred_element_type=F32).astype(BF16)
            both = jnp.concatenate([parts[:BR], parts[BR:]], axis=1)
            out = jnp.dot(total.astype(BF16), both, preferred_element_type=F32).astype(BF16)
            send[0, q, i] = out[:, :BR]
            send[1, q, i] = out[:, BR:]
            return 0

        lax.fori_loop(0, CAP, one, 0, unroll=True)
        copy(0, dx, dy).start()
        copy(1, dx, dy).start()
    for h in range(2):
        for d in range(SIDE):
            meta_copy(h, d).wait()
        for dx in range(SIDE):
            for dy in range(SIDE):
                copy(h, dx, dy).wait()


def grid_send(blk, slot, vis, target, weight):
    width = vis.shape[-1]
    any_space = pl.BlockSpec(memory_space=pl.ANY)
    vmem = pl.BlockSpec(memory_space=pltpu.VMEM)
    nb = vis.shape[0]
    return pl.pallas_call(
        grid_send_kernel,
        out_shape=(
            jax.ShapeDtypeStruct((2, SIDE, SIDE, CAP, TC, width), BF16),
            jax.ShapeDtypeStruct((2 * SIDE, N_OWN, 128), jnp.int32),
        ),
        in_specs=[pl.BlockSpec(memory_space=pltpu.SMEM), vmem, vmem, vmem, vmem, vmem],
        out_specs=(any_space, any_space),
        scratch_shapes=[
            pltpu.VMEM((2, N_OWN, CAP, TC, width), BF16),
            pltpu.SemaphoreType.DMA((2, SIDE, SIDE)),
            pltpu.SemaphoreType.DMA((2, SIDE, SIDE)),
            pltpu.SemaphoreType.DMA((2, SIDE)),
            pltpu.SemaphoreType.DMA((2 * SIDE,)),
            pltpu.SemaphoreType.DMA((2 * SIDE,)),
            pltpu.SemaphoreType.DMA((2,)),
        ],
        compiler_params=pltpu.CompilerParams(collective_id=0, has_side_effects=True, vmem_limit_bytes=48 * MIB),
        name="grid_send",
    )(blk, slot, vis, target, weight, jnp.asarray(split_constant()))


def sum_kernel(meta, rec, out, acc):
    g = pl.program_id(0)
    h, off = g // SIDE, lax.rem(g, SIDE)
    uv = lax.axis_index("uv")
    x, y = uv // SIDE, lax.rem(uv, SIDE)
    shifted_x, shifted_y = lax.rem(x + off, SIDE), lax.rem(y + off, SIDE)
    owner = jnp.where(h == 0, x * SIDE + shifted_y, shifted_x * SIDE + y)
    acc[...] = jnp.zeros_like(acc)
    for d in range(SIDE):
        for i in range(CAP):
            s = meta[h * SIDE + d, owner, i]
            acc[s] = acc[s] + rec[0, 0, d, i].astype(F32)
    out[0, 0] = acc[:SLOTS].astype(BF16)


def sum_slots(meta, rec):
    width = rec.shape[-1]
    return pl.pallas_call(
        sum_kernel,
        grid=(2 * SIDE,),
        out_shape=jax.ShapeDtypeStruct((2, SIDE, SLOTS, TC, width), BF16),
        in_specs=[
            pl.BlockSpec(memory_space=pltpu.SMEM),
            pl.BlockSpec((1, 1, SIDE, CAP, TC, width), lambda g: (g // SIDE, g % SIDE, 0, 0, 0, 0)),
        ],
        out_specs=pl.BlockSpec((1, 1, SLOTS, TC, width), lambda g: (g // SIDE, g % SIDE, 0, 0, 0)),
        scratch_shapes=[pltpu.VMEM((SLOTS + 1, TC, width), F32)],
        compiler_params=pltpu.CompilerParams(vmem_limit_bytes=24 * MIB),
        name="sum_slots",
    )(meta, rec)


def delay_kernel(
    n_chan, part, table, galaxy, cube, power,
    got, piece, flat, table_vm, mine, others,
    send_sem, recv_sem, local_sem, zsend, zrecv, zlocal, psend, precv, table_sem,
):
    uv, chan = lax.axis_index("uv"), lax.axis_index("chan")
    rows = TC // n_chan

    def z_peer(d):
        return (uv, lax.rem(chan + d, n_chan))

    load_table = pltpu.make_async_copy(table, table_vm, table_sem)
    load_table.start()
    barrier = pltpu.get_barrier_semaphore()
    for d in range(1, SIDE):
        pl.semaphore_signal(barrier, inc=1, device_id=peer(uv, chan, dx=d), device_id_type=MESH)
        pl.semaphore_signal(barrier, inc=1, device_id=peer(uv, chan, dy=d), device_id_type=MESH)
    for d in range(1, n_chan):
        pl.semaphore_signal(barrier, inc=1, device_id=z_peer(d), device_id_type=MESH)
    pl.semaphore_wait(barrier, 2 * (SIDE - 1) + n_chan - 1)

    def copy(h, d):
        if d == 0:
            return pltpu.make_async_copy(part.at[h, d], got.at[h, d], local_sem.at[h])
        device = peer(uv, chan, dy=d) if h == 0 else peer(uv, chan, dx=d)
        return pltpu.make_async_remote_copy(
            part.at[h, d], got.at[h, d], send_sem.at[h, d], recv_sem.at[h, d], device_id=device, device_id_type=MESH
        )

    for d in (2, 1, 3, 0):
        for h in range(2):
            copy(h, d).start()
    for h in range(2):
        for d in range(SIDE):
            copy(h, d).wait()

    width = got.shape[-1]

    def one_slot(s, _):
        for h in range(2):
            total = got[h, 0, s].astype(F32)
            for d in range(1, SIDE):
                total = total + got[h, d, s].astype(F32)
            piece[:, s, :, h * width : (h + 1) * width] = total.astype(BF16).reshape(n_chan, rows, width)
        return 0

    lax.fori_loop(0, SLOTS, one_slot, 0)

    def z_copy(d):
        there, _ = lax.rem(chan + d, n_chan), None
        columns = pl.ds(pl.multiple_of(chan * 2 * width, 2 * width), 2 * width)
        if d == 0:
            return pltpu.make_async_copy(piece.at[there], flat.at[:, :, columns], zlocal)
        return pltpu.make_async_remote_copy(
            piece.at[there], flat.at[:, :, columns], zsend.at[d], zrecv.at[d],
            device_id=z_peer(d), device_id_type=MESH,
        )

    for d in (*range(1, n_chan), 0):
        z_copy(d).start()
    for d in range(n_chan):
        z_copy(d).wait()
    load_table.wait()

    step = 256
    x = flat[...].reshape(SLOTS * rows, 2 * CH)
    for c in range(CH // step):
        lo = slice(c * step, (c + 1) * step)
        hi = slice(CH + c * step, CH + (c + 1) * step)
        re = jnp.dot(x, table_vm[:, lo], preferred_element_type=F32).reshape(SLOTS, rows, step)
        im = jnp.dot(x, table_vm[:, hi], preferred_element_type=F32).reshape(SLOTS, rows, step)
        cube[:, :, lo] = re.astype(BF16)
        cube[:, :, hi] = im.astype(BF16)
        product = re * galaxy[:, :, lo].astype(F32) + im * galaxy[:, :, hi].astype(F32)
        mine[:, lo] = jnp.sum(product, axis=1)

    def p_copy(d):
        return pltpu.make_async_remote_copy(
            mine, others.at[d - 1], psend.at[d - 1], precv.at[d - 1], device_id=z_peer(d), device_id_type=MESH
        )

    for d in range(1, n_chan):
        p_copy(d).start()
    for d in range(1, n_chan):
        p_copy(d).wait()
    total = mine[...]
    for d in range(n_chan - 1):
        total = total + others[d]
    power[...] = total / F32(math.sqrt(TC))


def delay_power(n_chan, part, galaxy):
    width = part.shape[-1]
    rows = TC // n_chan
    vmem = pl.BlockSpec(memory_space=pltpu.VMEM)
    any_space = pl.BlockSpec(memory_space=pl.ANY)
    dma = pltpu.SemaphoreType.DMA
    return pl.pallas_call(
        functools.partial(delay_kernel, n_chan),
        out_shape=(
            jax.ShapeDtypeStruct((SLOTS, rows, 2 * CH), BF16),
            jax.ShapeDtypeStruct((SLOTS, CH), F32),
        ),
        in_specs=[any_space, any_space, vmem],
        out_specs=(vmem, vmem),
        scratch_shapes=[
            pltpu.VMEM((2, SIDE, SLOTS, TC, width), BF16),
            pltpu.VMEM((n_chan, SLOTS, rows, 2 * width), BF16),
            pltpu.VMEM((SLOTS, rows, 2 * CH), BF16),
            pltpu.VMEM((2 * CH, 2 * CH), BF16),
            pltpu.VMEM((SLOTS, CH), F32),
            pltpu.VMEM((n_chan - 1, SLOTS, CH), F32),
            dma((2, SIDE)),
            dma((2, SIDE)),
            dma((2,)),
            dma((n_chan,)),
            dma((n_chan,)),
            dma,
            dma((n_chan - 1,)),
            dma((n_chan - 1,)),
            dma,
        ],
        compiler_params=pltpu.CompilerParams(collective_id=1, has_side_effects=True, vmem_limit_bytes=48 * MIB),
        name="delay_power",
    )(part, jnp.asarray(table_constant(n_chan)), galaxy)


def solution(mesh):
    n_chan = mesh.shape["chan"]

    def body(vis, row_cell, tap_weight, tap_offset, block_tile, tile_owner, galaxy):
        nb = block_tile.shape[0]
        blk, slot = block_lists(block_tile, tile_owner)
        blocks = vis.reshape(nb, 2 * BR, vis.shape[2])
        target = row_cell.reshape(nb, 1, BR) + tap_offset[None, :, None]
        weight = jnp.transpose(tap_weight.reshape(KT, nb, BR), (1, 0, 2)).astype(F32)
        rec, meta = grid_send(blk, slot, blocks, target, weight)
        part = sum_slots(meta, rec)
        return delay_power(n_chan, part, galaxy)

    return jax.shard_map(
        body,
        mesh=mesh,
        in_specs=(
            P("uv", None, "chan"),
            P("uv"),
            P(None, "uv"),
            P(),
            P("uv"),
            P(),
            P("uv", "chan", None),
        ),
        out_specs=(P("uv", "chan", None), P("uv", None)),
        check_vma=False,
    )
```

time: 379 us -> 164 us (0.43); the launches traced: 374 us -> 164 us
  waiting for transfers between devices: 174 us -> 0 us
  Pallas kernels: 0 us -> 151 us
  local copies, waits for them, and re-layouts: 63.7 us -> 10.4 us
  matrix products: 52.2 us -> 0 us
  starting transfers between devices: 36.5 us -> 0 us
  other arithmetic: 29.6 us -> 1.87 us
  blocking collectives: 16.8 us -> 0 us
    all_to_all x5 -> x0, waiting for transfers between devices: 174 us -> none  [the longest x1 169 us: body(): lax.all_to_all(sent_vis, 'uv', split_axis=0, concat_axis=0, tiled=True)]
    pallas_call x0 -> x4, Pallas kernels: none -> 151 us  [the longest x1 75.9 us: grid_send(): pl.pallas_call(grid_send_kernel, out_shape=(jax.ShapeDtypeStruct((2, SIDE...]
    dot_general x3 -> x0, matrix products: 52.2 us -> none  [the longest x1 26.9 us: body(): jnp.einsum('bs,bcf->scf', pick, contrib, precision=lax.Precision.HIGHEST)]
    all_to_all x5 -> x0, starting transfers between devices: 36.5 us -> none  [the longest x1 12 us: body(): lax.all_to_all(gridded, 'chan', split_axis=1, concat_axis=3, tiled=True)]
    scatter x4 -> x0, local copies, waits for them, and re-layouts: 30.1 us -> none  [the longest x1 17.7 us: body(): jnp.zeros((buffer_size, BR, 2 * chan_dev), jnp.bfloat16).at[place]]
    another operation x6 -> x0, other arithmetic: 19.9 us -> none
    all_to_all x1 -> x0, blocking collectives: 16.8 us -> none  [from_everyone(): lax.all_to_all(jnp.broadcast_to(x[None], (size, *x.shape)), axis, 0, 0, t...]
    reshape x2 -> x0, local copies, waits for them, and re-layouts: 13.6 us -> none  [the longest x1 10.8 us: body(): blocks = vis.reshape(nblocks, BR, 2 * chan_dev)]
  transfers between devices with their start and end apart: 5 -> 0, of which waited for: 2 -> 0; matrix products, arithmetic and copies ran while one was open for 20% -> 0% of each run, Pallas kernels for 0% -> 0%
where the time goes in v1:
time: 164 us
  Pallas kernels  151 us (92%)
  local copies, waits for them, and re-layouts  10.4 us (6%)
  other arithmetic  1.87 us (1%)
    pallas_call x1, Pallas kernels, grid_send(): pl.pallas_call(grid_send_kernel, out_shape=(jax.ShapeDtypeStruct((2, SIDE...  75.9 us
    pallas_call x1, Pallas kernels, delay_power(): pl.pallas_call(functools.partial(delay_kernel, n_chan), out_shape=(jax.Sh...  64.7 us
    unnamed x14, local copies, waits for them, and re-layouts  10.4 us
    pallas_call x1, Pallas kernels, sum_slots(): pl.pallas_call(sum_kernel, grid=(2 * SIDE,), out_shape=jax.ShapeDtypeStru...  5.72 us
    pallas_call x1, Pallas kernels, block_lists(): pl.pallas_call(lists_kernel, out_shape=(table, table), in_specs=[smem, sm...  4.75 us

profile of v1, /device:TPU:1, one launch (start us, length us, event | category | flops | bytes accessed | tf_op | source)
XLA Modules:
  0.0 164.0 jit_solution(5694309264216518210)
XLA Ops:
  0.6 4.8 %block_lists.1 = (s32[16,128]{1,0:T(8,128)}, s32[16,128]{1,0:T(8,128)}) custom-call(s32[96]{0:T(128)} %block_tile.1, s32[160]{0:T(256)} %tile_owner.1), custom_call_target="tpu_custom_call" | custom-call | tf_op jit(solution)/shard_map/block_lists/pallas_call | solution.py:93
  5.4 0.9 broadcast_add_fusion.target
  6.3 1.0 convert_bitcast_fusion.weight
  7.3 0.0 copy-start.3
  7.3 0.9 copy-done.3
  8.2 0.0 copy-start.4
  8.2 0.7 copy-done.4
  8.9 0.0 copy-start.5
  8.9 0.7 copy-done.5
  9.6 75.9 %grid_send.1 = (bf16[2,4,4,11,128,128]{5,4,3,2,1,0:T(8,128)(2,1)}, s32[8,16,128]{2,1,0:T(8,128)S(1)}) custom-call(s32[16,128]{1,0:T(8,128)S(1)} %copy-done.4, s32[16,128]{1,0:T(8,128)S(1)} %copy-done.5, bf16[96,256,128]{2,1,0:T(8,128)(2,1)} %bitcast.7, s32[96,8,128]{2,1,0:T(8,128)S(1)} %broadcast_add_fusion.target, ...), custom_call_target="tpu_custom_call" | custom-call | tf_op jit(solution)/shard_map/grid_send/pallas_call | solution.py:176
  85.4 0.0 copy-start.1
  85.5 4.3 %copy-done.1 = bf16[2,4,4,11,128,128]{5,4,3,2,1,0:T(8,128)(2,1)S(1)} copy-done((bf16[2,4,4,11,128,128]{5,4,3,2,1,0:T(8,128)(2,1)S(1)}, bf16[2,4,4,11,128,128]{5,4,3,2,1,0:T(8,128)(2,1)}, u32[]{:S(2)}) %copy-start.1) | copy-done | bytes 11534360
  89.7 0.0 copy-start.2
  89.7 5.7 %sum_slots.1.part = bf16[2,4,19,128,128]{4,3,2,1,0:T(8,128)(2,1)S(1)} custom-call(s32[8,16,128]{2,1,0:T(8,128)S(1)} %get-tuple-element.8.meta, bf16[2,4,4,11,128,128]{5,4,3,2,1,0:T(8,128)(2,1)S(1)} %copy-done.1), custom_call_target="tpu_custom_call" | custom-call | tf_op jit(solution)/shard_map/sum_slots/pallas_call | solution.py:215
  95.5 0.0 copy-start
  95.5 2.2 %copy-done = bf16[2,4,19,128,128]{4,3,2,1,0:T(8,128)(2,1)} copy-done((bf16[2,4,19,128,128]{4,3,2,1,0:T(8,128)(2,1)}, bf16[2,4,19,128,128]{4,3,2,1,0:T(8,128)(2,1)S(1)}, u32[]{:S(2)}) %copy-start) | copy-done | bytes 4980760
  97.7 0.0 copy-done.2
  97.7 64.7 %delay_power.1 = (bf16[19,16,2048]{2,1,0:T(8,128)(2,1)S(1)}, f32[19,1024]{1,0:T(8,128)S(1)}) custom-call(bf16[2,4,19,128,128]{4,3,2,1,0:T(8,128)(2,1)} %copy-done, bf16[2048,2048]{1,0:T(8,128)(2,1)} %constant.5.clone.table, bf16[19,16,2048]{2,1,0:T(8,128)(2,1)S(1)} %copy-done.2), custom_call_target="tpu_custom_call" | custom-call | tf_op jit(solution)/shard_map/delay_power/pallas_call | solution.py:327
  162.4 1.0 copy.13
  163.4 0.6 copy.14
Async XLA Ops:
  7.3 0.9 copy-start.3
  8.2 0.7 copy-start.4
  8.9 0.7 copy-start.5
  85.4 4.3 %copy-start.1 = (bf16[2,4,4,11,128,128]{5,4,3,2,1,0:T(8,128)(2,1)S(1)}, bf16[2,4,4,11,128,128]{5,4,3,2,1,0:T(8,128)(2,1)}, u32[]{:S(2)}) copy-start(bf16[2,4,4,11,128,128]{5,4,3,2,1,0:T(8,128)(2,1)} %get-tuple-element.9.rec) | copy-start | bytes 34603012
  89.7 7.9 %copy-start.2 = (bf16[19,16,2048]{2,1,0:T(8,128)(2,1)S(1)}, bf16[19,16,2048]{2,1,0:T(8,128)(2,1)}, u32[]{:S(2)}) copy-start(bf16[19,16,2048]{2,1,0:T(8,128)(2,1)} %galaxy.1) | copy-start | bytes 3735556
  95.5 2.2 %copy-start = (bf16[2,4,19,128,128]{4,3,2,1,0:T(8,128)(2,1)}, bf16[2,4,19,128,128]{4,3,2,1,0:T(8,128)(2,1)S(1)}, u32[]{:S(2)}) copy-start(bf16[2,4,19,128,128]{4,3,2,1,0:T(8,128)(2,1)S(1)} %sum_slots.1.part) | copy-start | bytes 14942212

commit v2 on v0

v2 whole, which is shorter than its diff:
```python
import functools
import math

import jax
import jax.numpy as jnp
import numpy as np
from jax import lax
from jax.experimental import pallas as pl
from jax.experimental.pallas import tpu as pltpu
from jax.sharding import PartitionSpec as P

MESH = pl.DeviceIdType.MESH
CH = 1024
BR = 128
TC = 128
KT = 8
N_OWN = 16
CAP = 11
SLOTS = 19
BLOCKS = 96
TILES = 160
SIDE = 4
ORDER = (2, 1, 3, 0)
F32 = jnp.float32
BF16 = jnp.bfloat16
MIB = 2**20


def table_constant(n_chan):
    freq = np.arange(CH, dtype=np.int64)
    phase = ((freq[:, None] * freq[None, :]) % CH).astype(np.float32) * np.float32(2.0 * math.pi / CH)
    cosine, sine = np.cos(phase), np.sin(phase)
    x = freq.astype(np.float32) * np.float32(2.0 * math.pi / CH)
    taper = (
        np.float32(0.35875)
        - np.float32(0.48829) * np.cos(x)
        + np.float32(0.14128) * np.cos(np.float32(2.0) * x)
        - np.float32(0.01168) * np.cos(np.float32(3.0) * x)
    )
    scale = (taper / np.float32(math.sqrt(CH)))[:, None]
    upper = np.concatenate([cosine * scale, -sine * scale], axis=1)
    lower = np.concatenate([sine * scale, cosine * scale], axis=1)
    table = np.stack([upper, lower]).reshape(2, n_chan, CH // n_chan, 2 * CH)
    return table.transpose(1, 0, 2, 3).reshape(2 * CH, 2 * CH).astype(jnp.bfloat16)


def split_constant():
    p = np.zeros((2 * BR, 2 * BR), np.float32)
    r = np.arange(BR)
    p[r, 2 * r] = 1.0
    p[BR + r, 2 * r + 1] = 1.0
    return p.astype(jnp.bfloat16)


def peer(uv, chan, dx=0, dy=0):
    x = lax.rem(uv // SIDE + dx, SIDE)
    y = lax.rem(lax.rem(uv, SIDE) + dy, SIDE)
    return (x * SIDE + y, chan)


def column(row):
    return jnp.transpose(jnp.broadcast_to(row, (128, 128)))


def tall(row):
    return jnp.concatenate([column(row[:, :128]), column(row[:, 128:])], axis=0)


def position_in_order(d):
    return jnp.where(d == 2, 0, jnp.where(d == 1, 1, jnp.where(d == 3, 2, 3)))


def count(mask):
    return jnp.where(mask, 1, 0)


def make_tables(x, y, tb, lists, places):
    tile_r, own_r = tb[0:1, :128], tb[1:2, :]
    lane = lax.broadcasted_iota(jnp.int32, (128, 128), 1)
    sub = lax.broadcasted_iota(jnp.int32, (128, 128), 0)
    tile_c = column(tile_r)
    lane_t = lax.broadcasted_iota(jnp.int32, (256, 128), 1)
    t_c = lax.broadcasted_iota(jnp.int32, (256, 128), 0)
    own_c = tall(own_r)
    match = tile_r == t_c
    number_c = jnp.sum(count(match), axis=1, keepdims=True)
    number_r = [jnp.sum(count(tile_c == lane + 128 * i), axis=0, keepdims=True) for i in range(2)]
    same = [own_r[:, 128 * i : 128 * (i + 1)] == own_c for i in range(2)]
    rank_c = sum(jnp.sum(count(same[i] & (lane_t + 128 * i < t_c)), axis=1, keepdims=True) for i in range(2))
    earlier_r = jnp.sum(count((tile_c == tile_r) & (sub < lane)), axis=0, keepdims=True)
    repeat_c = count(column(earlier_r) > 0)
    dx_c, dy_c = ((own_c >> 2) - x) & 3, ((own_c & 3) - y) & 3
    slot_key = jnp.where(t_c < TILES, own_c * 32 + rank_c, -1)
    start_c = sum(
        jnp.sum(jnp.where(same[i] & (lane_t + 128 * i < t_c), number_r[i], 0), axis=1, keepdims=True) for i in range(2)
    )
    last_c = jnp.where(number_c > 0, start_c + number_c, 0)
    for i in range(4):
        hit = slot_key == lane_t + 128 * i
        places[i : i + 1, :] = jnp.sum(jnp.where(hit, last_c, 0), axis=0, keepdims=True) - 1
    for h in range(2):
        group_c, inner_c = (dx_c, dy_c) if h == 0 else (dy_c, dx_c)
        first_c = group_c * 64 + position_in_order(inner_c) * CAP + start_c
        key_r = jnp.sum(jnp.where(match, first_c, 0), axis=0, keepdims=True) + earlier_r
        key_c = column(jnp.where(lane[0:1] < BLOCKS, key_r, -1))
        for i in range(2):
            hit = key_c == lane + 128 * i
            row = 4 * h + i
            lists[row : row + 1, :] = jnp.sum(jnp.where(hit, sub, 0), axis=0, keepdims=True)
            lists[row + 2 : row + 3, :] = jnp.sum(jnp.where(hit, repeat_c, 0), axis=0, keepdims=True)


def kernel(
    n_chan, cuts,
    block_tile, tile_owner, tap_offset, cells, weight, split, vis_hbm, table_hbm, galaxy_hbm,
    cube, power,
    vis, table, galaxy, tb, lists, places, lists_sm, places_sm, carry, send, rec0, rec1, rec2, rec3, part, got, piece, flat,
    mine, shares, total_power,
    load_sem, msend, mrecv, sm_sem, asend, arecv, bsend, brecv, zsend, zrecv, zlocal, psend, precv, gsend, grecv,
):
    uv, chan = lax.axis_index("uv"), lax.axis_index("chan")
    x, y = uv // SIDE, lax.rem(uv, SIDE)
    rows = TC // n_chan
    width = vis.shape[-1]
    recs = (rec0, rec1, rec2, rec3)

    def z_peer(d):
        return (uv, lax.rem(chan + d, n_chan))

    def xy_peer(h, d):
        return peer(uv, chan, dx=d) if h == 0 else peer(uv, chan, dy=d)

    loads = [
        pltpu.make_async_copy(vis_hbm, vis, load_sem.at[0]),
        pltpu.make_async_copy(table_hbm, table, load_sem.at[1]),
        pltpu.make_async_copy(galaxy_hbm, galaxy, load_sem.at[2]),
    ]
    loads[0].start()
    barrier = pltpu.get_barrier_semaphore()
    for h in range(2):
        for d in range(1, SIDE):
            pl.semaphore_signal(barrier, inc=1, device_id=xy_peer(h, d), device_id_type=MESH)
    for d in range(1, n_chan):
        pl.semaphore_signal(barrier, inc=1, device_id=z_peer(d), device_id_type=MESH)

    tb[...] = jnp.full(tb.shape, -1, jnp.int32)
    tb[0:1, 0 : block_tile.shape[1]] = block_tile[...]
    tb[1:2, 0 : tile_owner.shape[1]] = tile_owner[...]
    make_tables(x, y, tb, lists, places.at[0])
    places[SIDE] = places[0]
    to_scalars = pltpu.make_async_copy(lists, lists_sm, sm_sem.at[0])
    to_scalars.start()
    pl.semaphore_wait(barrier, 2 * (SIDE - 1) + n_chan - 1)

    def places_copy(h, d):
        k = h * SIDE + d
        return pltpu.make_async_remote_copy(
            places.at[0], places.at[k], msend.at[k], mrecv.at[k], device_id=xy_peer(h, d), device_id_type=MESH
        )

    for h in range(2):
        for d in range(1, SIDE):
            if h == 0:
                places_copy(h, d).start()
    for d in range(1, SIDE):
        places_copy(1, d).start()
    carry[...] = jnp.zeros_like(carry)
    to_scalars.wait()
    loads[0].wait()
    loads[1].start()
    loads[2].start()

    def a_copy(h, g, k):
        n, size = cuts[k] // CAP, cuts[k + 1] - cuts[k]
        return pltpu.make_async_remote_copy(
            send.at[h, g - 1, pl.ds(cuts[k], size)], recs[n].at[h, g, pl.ds(cuts[k] - n * CAP, size)], asend.at[h, g - 1, k], arecv.at[h, g - 1, k],
            device_id=xy_peer(h, g), device_id_type=MESH,
        )

    cell_rows = lax.broadcasted_iota(jnp.int32, (TC, BR), 0)

    def place(n, p, _):
        for g in ORDER:
            for h in range(2):
                row, at = 4 * h + g // 2, 64 * (g % 2) + p
                b = jnp.minimum(lists_sm[row, at], BLOCKS - 1)
                keep = lists_sm[row + 2, at].astype(F32)
                away = cell_rows - cells[b]
                w = weight[b]
                matrix = jnp.zeros((TC, BR), F32)
                for k in range(KT):
                    matrix = matrix + jnp.where(away == tap_offset[k], w[k : k + 1, :], 0.0)
                half = jnp.dot(split[h], vis[b], preferred_element_type=F32).astype(BF16)
                out = jnp.dot(matrix.astype(BF16), half, preferred_element_type=F32)
                out = out + keep * carry[h, g]
                carry[h, g] = out
                if g == 0:
                    recs[n][h, 0, p - n * CAP] = out.astype(BF16)
                else:
                    send[h, g - 1, p] = out.astype(BF16)
        return 0

    n_cuts = len(cuts) - 1
    for k in range(n_cuts):
        lax.fori_loop(cuts[k], cuts[k + 1], functools.partial(place, cuts[k] // CAP), 0)
        for g in ORDER[:3]:
            for h in range(2):
                a_copy(h, g, k).start()

    for h in range(2):
        for d in range(1, SIDE):
            places_copy(h, d).wait()
    places_load = pltpu.make_async_copy(places, places_sm, sm_sem.at[1])
    places_load.start()
    places_load.wait()

    slot_cuts = (0, 10, SLOTS)

    def b_copy(h, off, q):
        cut = pl.ds(slot_cuts[q], slot_cuts[q + 1] - slot_cuts[q])
        return pltpu.make_async_remote_copy(
            part.at[h, off - 1, cut], got.at[h, off, cut], bsend.at[h, off - 1, q], brecv.at[h, off - 1, q],
            device_id=xy_peer(1 - h, off), device_id_type=MESH,
        )

    arrived = 0
    for n, off in enumerate(ORDER):
        needed = CAP * (n + 1)
        while cuts[arrived] < needed:
            for h in range(2):
                for g in range(1, SIDE):
                    a_copy(h, g, arrived).wait_recv()
            arrived += 1
        for h in range(2):
            ox = x if h == 0 else lax.rem(x + off, SIDE)
            oy = lax.rem(y + off, SIDE) if h == 0 else y

            def one(s, _, h=h, off=off, rec=recs[n], ox=ox, oy=oy):
                total = jnp.zeros((TC, width), F32)
                for d in range(SIDE):
                    p = places_sm[h * SIDE + d, ox, 32 * oy + s]
                    there = jnp.where(p >= 0, F32(1.0), F32(0.0))
                    at = jnp.clip(p, 0, CAP - 1)
                    total = total + there * rec[h, d, at].astype(F32)
                if off == 0:
                    got[h, 0, s] = total.astype(BF16)
                else:
                    part[h, off - 1, s] = total.astype(BF16)
                return 0

            lax.fori_loop(0, SLOTS, one, 0)
            if off:
                for q in range(2):
                    b_copy(h, off, q).start()

    def z_copy(d, q):
        there = lax.rem(chan + d, n_chan)
        columns = pl.ds(pl.multiple_of(chan * 2 * width, 2 * width), 2 * width)
        cut = pl.ds(slot_cuts[q], slot_cuts[q + 1] - slot_cuts[q])
        if d == 0:
            return pltpu.make_async_copy(piece.at[there, cut], flat.at[cut, :, columns], zlocal.at[q])
        return pltpu.make_async_remote_copy(
            piece.at[there, cut], flat.at[cut, :, columns], zsend.at[d - 1, q], zrecv.at[d - 1, q],
            device_id=z_peer(d), device_id_type=MESH,
        )

    def one_slot(s, _):
        for h in range(2):
            total = got[h, 0, s].astype(F32)
            for d in range(1, SIDE):
                total = total + got[h, d, s].astype(F32)
            piece[:, s, :, h * width : (h + 1) * width] = total.astype(BF16).reshape(n_chan, rows, width)
        return 0

    for q in range(2):
        for h in range(2):
            for off in range(1, SIDE):
                b_copy(h, off, q).wait_recv()
        lax.fori_loop(slot_cuts[q], slot_cuts[q + 1], one_slot, 0)
        for d in (*range(1, n_chan), 0):
            z_copy(d, q).start()
    loads[1].wait()
    loads[2].wait()

    step = 256
    for q in range(2):
        for d in range(n_chan):
            if d == 0:
                z_copy(d, q).wait()
            else:
                z_copy(d, q).wait_recv()
        lo_s, hi_s = slot_cuts[q], slot_cuts[q + 1]
        v = flat[lo_s:hi_s].reshape((hi_s - lo_s) * rows, 2 * CH)
        for c in range(CH // step):
            lo = slice(c * step, (c + 1) * step)
            hi = slice(CH + c * step, CH + (c + 1) * step)
            re = jnp.dot(v, table[:, lo], preferred_element_type=F32).reshape(hi_s - lo_s, rows, step)
            im = jnp.dot(v, table[:, hi], preferred_element_type=F32).reshape(hi_s - lo_s, rows, step)
            cube[lo_s:hi_s, :, lo] = re.astype(BF16)
            cube[lo_s:hi_s, :, hi] = im.astype(BF16)
            product = re * galaxy[lo_s:hi_s, :, lo].astype(F32) + im * galaxy[lo_s:hi_s, :, hi].astype(F32)
            mine[lo_s:hi_s, lo] = jnp.sum(product, axis=1)

    share = CH // n_chan

    def share_columns(c):
        return pl.ds(pl.multiple_of(c * share, share), share)

    def p_copy(d):
        return pltpu.make_async_remote_copy(
            mine.at[:, share_columns(lax.rem(chan + d, n_chan))], shares.at[d - 1], psend.at[d - 1], precv.at[d - 1],
            device_id=z_peer(d), device_id_type=MESH,
        )

    def g_copy(d):
        own = total_power.at[:, share_columns(chan)]
        return pltpu.make_async_remote_copy(
            own, own, gsend.at[d - 1], grecv.at[d - 1], device_id=z_peer(d), device_id_type=MESH
        )

    for d in range(1, n_chan):
        p_copy(d).start()
    total = mine[:, share_columns(chan)]
    for d in range(1, n_chan):
        p_copy(d).wait_recv()
        total = total + shares[d - 1]
    total_power[:, share_columns(chan)] = total / F32(math.sqrt(TC))
    for d in range(1, n_chan):
        g_copy(d).start()
    for h in range(2):
        for g in range(1, SIDE):
            for k in range(n_cuts):
                a_copy(h, g, k).wait_send()
            for q in range(2):
                b_copy(h, g, q).wait_send()
    for d in range(1, n_chan):
        for q in range(2):
            z_copy(d, q).wait_send()
        p_copy(d).wait_send()
    for d in range(1, n_chan):
        g_copy(d).wait()
    power[...] = total_power[...]


def fused(n_chan, cuts, block_tile, tile_owner, tap_offset, cells, weight, vis, galaxy):
    nb, _, width = vis.shape
    n_cuts = len(cuts) - 1
    rows = TC // n_chan
    smem = pl.BlockSpec(memory_space=pltpu.SMEM)
    vmem = pl.BlockSpec(memory_space=pltpu.VMEM)
    hbm = pl.BlockSpec(memory_space=pl.ANY)
    dma = pltpu.SemaphoreType.DMA
    return pl.pallas_call(
        functools.partial(kernel, n_chan, cuts),
        out_shape=(
            jax.ShapeDtypeStruct((SLOTS, rows, 2 * CH), BF16),
            jax.ShapeDtypeStruct((SLOTS, CH), F32),
        ),
        in_specs=[vmem, vmem, smem, vmem, vmem, vmem, hbm, hbm, hbm],
        out_specs=(vmem, vmem),
        scratch_shapes=[
            pltpu.VMEM(vis.shape, BF16),
            pltpu.VMEM((2 * CH, 2 * CH), BF16),
            pltpu.VMEM(galaxy.shape, BF16),
            pltpu.VMEM((8, 256), jnp.int32),
            pltpu.VMEM((8, 128), jnp.int32),
            pltpu.VMEM((2 * SIDE, 8, 128), jnp.int32),
            pltpu.SMEM((8, 128), jnp.int32),
            pltpu.SMEM((2 * SIDE, 8, 128), jnp.int32),
            pltpu.VMEM((2, SIDE, TC, width), F32),
            pltpu.VMEM((2, SIDE - 1, SIDE * CAP, TC, width), BF16),
            *[pltpu.VMEM((2, SIDE, CAP, TC, width), BF16) for _ in range(SIDE)],
            pltpu.VMEM((2, SIDE - 1, SLOTS, TC, width), BF16),
            pltpu.VMEM((2, SIDE, SLOTS, TC, width), BF16),
            pltpu.VMEM((n_chan, SLOTS, rows, 2 * width), BF16),
            pltpu.VMEM((SLOTS, rows, 2 * CH), BF16),
            pltpu.VMEM((SLOTS, CH), F32),
            pltpu.VMEM((n_chan - 1, SLOTS, CH // n_chan), F32),
            pltpu.VMEM((SLOTS, CH), F32),
            dma((3,)),
            dma((2 * SIDE,)),
            dma((2 * SIDE,)),
            dma((2,)),
            dma((2, SIDE - 1, n_cuts)),
            dma((2, SIDE - 1, n_cuts)),
            dma((2, SIDE - 1, 2)),
            dma((2, SIDE - 1, 2)),
            dma((n_chan - 1, 2)),
            dma((n_chan - 1, 2)),
            dma((2,)),
            dma((n_chan - 1,)),
            dma((n_chan - 1,)),
            dma((n_chan - 1,)),
            dma((n_chan - 1,)),
        ],
        compiler_params=pltpu.CompilerParams(collective_id=0, has_side_effects=True, vmem_limit_bytes=60 * MIB),
        name="grid_delay",
    )(
        block_tile.reshape(1, -1), tile_owner.reshape(1, -1), tap_offset, cells, weight,
        jnp.asarray(split_constant().reshape(2, BR, 2 * BR)), vis, jnp.asarray(table_constant(n_chan)), galaxy,
    )


def solution(mesh):
    n_chan = mesh.shape["chan"]

    def body(vis, row_cell, tap_weight, tap_offset, block_tile, tile_owner, galaxy):
        nb = block_tile.shape[0]
        blocks = vis.reshape(nb, 2 * BR, vis.shape[2])
        cells = row_cell.reshape(nb, 1, BR)
        weight = jnp.transpose(tap_weight.reshape(KT, nb, BR), (1, 0, 2)).astype(F32)
        return fused(
            n_chan, (0, 3, 11, 22, 33, 44), block_tile, tile_owner, tap_offset, cells, weight, blocks, galaxy
        )

    return jax.shard_map(
        body,
        mesh=mesh,
        in_specs=(
            P("uv", None, "chan"),
            P("uv"),
            P(None, "uv"),
            P(),
            P("uv"),
            P(),
            P("uv", "chan", None),
        ),
        out_specs=(P("uv", "chan", None), P("uv", None)),
        check_vma=False,
    )
```

time: 379 us -> 145 us (0.38); the launches traced: 374 us -> 145 us
  waiting for transfers between devices: 174 us -> 0 us
  Pallas kernels: 0 us -> 139 us
  local copies, waits for them, and re-layouts: 63.7 us -> 3.14 us
  matrix products: 52.2 us -> 0 us
  starting transfers between devices: 36.5 us -> 0 us
  other arithmetic: 29.6 us -> 1.7 us
  blocking collectives: 16.8 us -> 0 us
    all_to_all x5 -> x0, waiting for transfers between devices: 174 us -> none  [the longest x1 169 us: body(): lax.all_to_all(sent_vis, 'uv', split_axis=0, concat_axis=0, tiled=True)]
    pallas_call x0 -> x1, Pallas kernels: none -> 139 us  [fused(): pl.pallas_call(functools.partial(kernel, n_chan, cuts), out_shape=(jax.Sh...]
    dot_general x3 -> x0, matrix products: 52.2 us -> none  [the longest x1 26.9 us: body(): jnp.einsum('bs,bcf->scf', pick, contrib, precision=lax.Precision.HIGHEST)]
    all_to_all x5 -> x0, starting transfers between devices: 36.5 us -> none  [the longest x1 12 us: body(): lax.all_to_all(gridded, 'chan', split_axis=1, concat_axis=3, tiled=True)]
    scatter x4 -> x0, local copies, waits for them, and re-layouts: 30.1 us -> none  [the longest x1 17.7 us: body(): jnp.zeros((buffer_size, BR, 2 * chan_dev), jnp.bfloat16).at[place]]
    another operation x6 -> x0, other arithmetic: 19.9 us -> none
    all_to_all x1 -> x0, blocking collectives: 16.8 us -> none  [from_everyone(): lax.all_to_all(jnp.broadcast_to(x[None], (size, *x.shape)), axis, 0, 0, t...]
    reshape x2 -> x0, local copies, waits for them, and re-layouts: 13.6 us -> none  [the longest x1 10.8 us: body(): blocks = vis.reshape(nblocks, BR, 2 * chan_dev)]
  transfers between devices with their start and end apart: 5 -> 0, of which waited for: 2 -> 0; matrix products, arithmetic and copies ran while one was open for 20% -> 0% of each run, Pallas kernels for 0% -> 0%
where the time goes in v2:
time: 145 us
  Pallas kernels  139 us (96%)
  local copies, waits for them, and re-layouts  3.14 us (2%)
  other arithmetic  1.7 us (1%)
    pallas_call x1, Pallas kernels, fused(): pl.pallas_call(functools.partial(kernel, n_chan, cuts), out_shape=(jax.Sh...  139 us
    unnamed x4, local copies, waits for them, and re-layouts  3.14 us

profile of v2, /device:TPU:1, one launch (start us, length us, event | category | flops | bytes accessed | tf_op | source)
XLA Modules:
  0.0 144.6 jit_solution(16803171617214315445)
XLA Ops:
  0.6 1.7 %convert_bitcast_fusion.weight = f32[96,8,128]{2,1,0:T(8,128)} fusion(bf16[8,12288]{1,0:T(8,128)(2,1)} %param.11), kind=kLoop, calls=%fused_computation | loop fusion | flops 98304 | bytes 589824 | tf_op jit(solution)/shard_map/convert_element_type | solution.py:411
  2.3 139.1 %grid_delay.1 = (bf16[19,16,2048]{2,1,0:T(8,128)(2,1)}, f32[19,1024]{1,0:T(8,128)}) custom-call(s32[1,96]{1,0:T(1,128)} %bitcast.12, s32[1,160]{1,0:T(1,128)} %bitcast.11, s32[8]{0:T(128)} %tap_offset.1, s32[96,1,128]{2,1,0:T(1,128)} %bitcast.10, f32[96,8,128]{2,1,0:T(8,128)} %convert_bitcast_fusion.weight, bf16[2,128,256]{2,1,0:T(8,128)(2,1)} %constant.4.clone.split, ...), custom_call_target="tpu_custom_call" | custom-call | tf_op jit(solution)/shard_map/grid_delay/pallas_call | solution.py:353
  141.4 0.0 copy-start
  141.4 2.5 %copy.13 = bf16[19,16,2048]{2,1,0:T(8,128)(2,1)} copy(bf16[19,16,2048]{2,1,0:T(8,128)(2,1)} %get-tuple-element.4) | data formatting | bytes 2490368
  143.9 0.0 copy-done
  143.9 0.6 copy.14
Async XLA Ops:
  141.4 2.5 %copy-start = (f32[19,1024]{1,0:T(8,128)S(1)}, f32[19,1024]{1,0:T(8,128)}, u32[]{:S(2)}) copy-start(f32[19,1024]{1,0:T(8,128)} %get-tuple-element.5) | copy-start | bytes 233476

commit v3 on v2

--- a/solution.py
+++ b/solution.py
@@ -42,14 +42,6 @@
     lower = np.concatenate([sine * scale, cosine * scale], axis=1)
     table = np.stack([upper, lower]).reshape(2, n_chan, CH // n_chan, 2 * CH)
     return table.transpose(1, 0, 2, 3).reshape(2 * CH, 2 * CH).astype(jnp.bfloat16)
-
-
-def split_constant():
-    p = np.zeros((2 * BR, 2 * BR), np.float32)
-    r = np.arange(BR)
-    p[r, 2 * r] = 1.0
-    p[BR + r, 2 * r + 1] = 1.0
-    return p.astype(jnp.bfloat16)
 
 
 def peer(uv, chan, dx=0, dy=0):
@@ -112,11 +104,11 @@
 
 def kernel(
     n_chan, cuts,
-    block_tile, tile_owner, tap_offset, cells, weight, split, vis_hbm, table_hbm, galaxy_hbm,
+    block_tile, tile_owner, tap_offset, cells, weight, vis_hbm, table_hbm, galaxy_hbm,
     cube, power,
-    vis, table, galaxy, tb, lists, places, lists_sm, places_sm, carry, send, rec0, rec1, rec2, rec3, part, got, piece, flat,
+    vis, wide, table, galaxy, tb, lists, places, lists_sm, places_sm, carry, send, rec0, rec1, rec2, rec3, part, via, got, piece, flat,
     mine, shares, total_power,
-    load_sem, msend, mrecv, sm_sem, asend, arecv, bsend, brecv, zsend, zrecv, zlocal, psend, precv, gsend, grecv,
+    load_sem, msend, mrecv, sm_sem, asend, arecv, bsend, brecv, vsend, vrecv, zsend, zrecv, zlocal, psend, precv, gsend, grecv,
 ):
     uv, chan = lax.axis_index("uv"), lax.axis_index("chan")
     x, y = uv // SIDE, lax.rem(uv, SIDE)
@@ -131,11 +123,18 @@
         return peer(uv, chan, dx=d) if h == 0 else peer(uv, chan, dy=d)
 
     loads = [
-        pltpu.make_async_copy(vis_hbm, vis, load_sem.at[0]),
-        pltpu.make_async_copy(table_hbm, table, load_sem.at[1]),
-        pltpu.make_async_copy(galaxy_hbm, galaxy, load_sem.at[2]),
+        pltpu.make_async_copy(table_hbm, table, load_sem.at[0]),
+        pltpu.make_async_copy(galaxy_hbm, galaxy, load_sem.at[1]),
     ]
-    loads[0].start()
+    quarter = BLOCKS // 4
+    vis_loads = [
+        pltpu.make_async_copy(
+            vis_hbm.at[pl.ds(i * quarter, quarter)], vis.at[pl.ds(i * quarter, quarter)], load_sem.at[2 + i]
+        )
+        for i in range(4)
+    ]
+    for load in vis_loads:
+        load.start()
     barrier = pltpu.get_barrier_semaphore()
     for h in range(2):
         for d in range(1, SIDE):
@@ -150,6 +149,19 @@
     places[SIDE] = places[0]
     to_scalars = pltpu.make_async_copy(lists, lists_sm, sm_sem.at[0])
     to_scalars.start()
+
+    def split(i, _):
+        for j in range(4):
+            b = 4 * i + j
+            wide[2 * BR * j : 2 * BR * (j + 1), :] = vis[b].astype(F32)
+            for part_of in range(2):
+                rows_of = wide[pl.ds(2 * BR * j + part_of, BR, stride=2), :]
+                vis[b, BR * part_of : BR * (part_of + 1), :] = rows_of.astype(BF16)
+        return 0
+
+    for i, load in enumerate(vis_loads):
+        load.wait()
+        lax.fori_loop(i * quarter // 4, (i + 1) * quarter // 4, split, 0)
     pl.semaphore_wait(barrier, 2 * (SIDE - 1) + n_chan - 1)
 
     def places_copy(h, d):
@@ -166,9 +178,8 @@
         places_copy(1, d).start()
     carry[...] = jnp.zeros_like(carry)
     to_scalars.wait()
-    loads[0].wait()
+    loads[0].start()
     loads[1].start()
-    loads[2].start()
 
     def a_copy(h, g, k):
         n, size = cuts[k] // CAP, cuts[k + 1] - cuts[k]
@@ -190,7 +201,7 @@
                 matrix = jnp.zeros((TC, BR), F32)
                 for k in range(KT):
                     matrix = matrix + jnp.where(away == tap_offset[k], w[k : k + 1, :], 0.0)
-                half = jnp.dot(split[h], vis[b], preferred_element_type=F32).astype(BF16)
+                half = vis[b, BR * h : BR * (h + 1), :]
                 out = jnp.dot(matrix.astype(BF16), half, preferred_element_type=F32)
                 out = out + keep * carry[h, g]
                 carry[h, g] = out
@@ -214,13 +225,23 @@
     places_load.start()
     places_load.wait()
 
-    slot_cuts = (0, 10, SLOTS)
+    slot_cuts = (0, 5, 10, 15, SLOTS)
+    n_slot_cuts = len(slot_cuts) - 1
+    middle = 10
 
     def b_copy(h, off, q):
         cut = pl.ds(slot_cuts[q], slot_cuts[q + 1] - slot_cuts[q])
-        return pltpu.make_async_remote_copy(
-            part.at[h, off - 1, cut], got.at[h, off, cut], bsend.at[h, off - 1, q], brecv.at[h, off - 1, q],
+        k = off // 2
+        return pltpu.make_async_remote_copy(
+            part.at[h, off - 1, cut], got.at[h, 1 + k, cut], bsend.at[h, k, q], brecv.at[h, k, q],
             device_id=xy_peer(1 - h, off), device_id_type=MESH,
+        )
+
+    def via_copy(h, k):
+        cut = pl.ds(middle * k, middle if k == 0 else SLOTS - middle)
+        return pltpu.make_async_remote_copy(
+            part.at[h, 1, cut], via.at[h, cut], vsend.at[h, k], vrecv.at[h, k],
+            device_id=xy_peer(1 - h, 1 if k == 0 else SIDE - 1), device_id_type=MESH,
         )
 
     arrived = 0
@@ -235,8 +256,8 @@
             ox = x if h == 0 else lax.rem(x + off, SIDE)
             oy = lax.rem(y + off, SIDE) if h == 0 else y
 
-            def one(s, _, h=h, off=off, rec=recs[n], ox=ox, oy=oy):
-                total = jnp.zeros((TC, width), F32)
+            def one(add, s, _, h=h, off=off, rec=recs[n], ox=ox, oy=oy):
+                total = via[h, s].astype(F32) if add else jnp.zeros((TC, width), F32)
                 for d in range(SIDE):
                     p = places_sm[h * SIDE + d, ox, 32 * oy + s]
                     there = jnp.where(p >= 0, F32(1.0), F32(0.0))
@@ -248,9 +269,16 @@
                     part[h, off - 1, s] = total.astype(BF16)
                 return 0
 
-            lax.fori_loop(0, SLOTS, one, 0)
-            if off:
-                for q in range(2):
+            if off in (0, 2):
+                lax.fori_loop(0, SLOTS, functools.partial(one, False), 0)
+                if off:
+                    via_copy(h, 0).start()
+                    via_copy(h, 1).start()
+            else:
+                via_copy(h, off // 2).wait_recv()
+                for q in range(n_slot_cuts):
+                    add = (slot_cuts[q] < middle) == (off == 1)
+                    lax.fori_loop(slot_cuts[q], slot_cuts[q + 1], functools.partial(one, add), 0)
                     b_copy(h, off, q).start()
 
     def z_copy(d, q):
@@ -266,30 +294,27 @@
 
     def one_slot(s, _):
         for h in range(2):
-            total = got[h, 0, s].astype(F32)
-            for d in range(1, SIDE):
-                total = total + got[h, d, s].astype(F32)
+            total = got[h, 0, s].astype(F32) + got[h, 1, s].astype(F32) + got[h, 2, s].astype(F32)
             piece[:, s, :, h * width : (h + 1) * width] = total.astype(BF16).reshape(n_chan, rows, width)
         return 0
 
-    for q in range(2):
+    for q in range(n_slot_cuts):
         for h in range(2):
-            for off in range(1, SIDE):
+            for off in (1, 3):
                 b_copy(h, off, q).wait_recv()
         lax.fori_loop(slot_cuts[q], slot_cuts[q + 1], one_slot, 0)
         for d in (*range(1, n_chan), 0):
             z_copy(d, q).start()
+    loads[0].wait()
     loads[1].wait()
-    loads[2].wait()
 
     step = 256
-    for q in range(2):
-        for d in range(n_chan):
-            if d == 0:
-                z_copy(d, q).wait()
-            else:
-                z_copy(d, q).wait_recv()
-        lo_s, hi_s = slot_cuts[q], slot_cuts[q + 1]
+    for lo_s, hi_s in ((0, middle), (middle, SLOTS)):
+        for q in range(n_slot_cuts):
+            if lo_s <= slot_cuts[q] < hi_s:
+                z_copy(0, q).wait()
+                for d in range(1, n_chan):
+                    z_copy(d, q).wait_recv()
         v = flat[lo_s:hi_s].reshape((hi_s - lo_s) * rows, 2 * CH)
         for c in range(CH // step):
             lo = slice(c * step, (c + 1) * step)
@@ -331,10 +356,12 @@
         for g in range(1, SIDE):
             for k in range(n_cuts):
                 a_copy(h, g, k).wait_send()
-            for q in range(2):
-                b_copy(h, g, q).wait_send()
-    for d in range(1, n_chan):
-        for q in range(2):
+        for k in range(2):
+            via_copy(h, k).wait_send()
+            for q in range(n_slot_cuts):
+                b_copy(h, 2 * k + 1, q).wait_send()
+    for d in range(1, n_chan):
+        for q in range(n_slot_cuts):
             z_copy(d, q).wait_send()
         p_copy(d).wait_send()
     for d in range(1, n_chan):
@@ -356,10 +383,11 @@
             jax.ShapeDtypeStruct((SLOTS, rows, 2 * CH), BF16),
             jax.ShapeDtypeStruct((SLOTS, CH), F32),
         ),
-        in_specs=[vmem, vmem, smem, vmem, vmem, vmem, hbm, hbm, hbm],
+        in_specs=[vmem, vmem, smem, vmem, vmem, hbm, hbm, hbm],
         out_specs=(vmem, vmem),
         scratch_shapes=[
             pltpu.VMEM(vis.shape, BF16),
+            pltpu.VMEM((4 * 2 * BR, width), F32),
             pltpu.VMEM((2 * CH, 2 * CH), BF16),
             pltpu.VMEM(galaxy.shape, BF16),
             pltpu.VMEM((8, 256), jnp.int32),
@@ -371,33 +399,36 @@
             pltpu.VMEM((2, SIDE - 1, SIDE * CAP, TC, width), BF16),
             *[pltpu.VMEM((2, SIDE, CAP, TC, width), BF16) for _ in range(SIDE)],
             pltpu.VMEM((2, SIDE - 1, SLOTS, TC, width), BF16),
-            pltpu.VMEM((2, SIDE, SLOTS, TC, width), BF16),
+            pltpu.VMEM((2, SLOTS, TC, width), BF16),
+            pltpu.VMEM((2, SIDE - 1, SLOTS, TC, width), BF16),
             pltpu.VMEM((n_chan, SLOTS, rows, 2 * width), BF16),
             pltpu.VMEM((SLOTS, rows, 2 * CH), BF16),
             pltpu.VMEM((SLOTS, CH), F32),
             pltpu.VMEM((n_chan - 1, SLOTS, CH // n_chan), F32),
             pltpu.VMEM((SLOTS, CH), F32),
-            dma((3,)),
+            dma((6,)),
             dma((2 * SIDE,)),
             dma((2 * SIDE,)),
             dma((2,)),
             dma((2, SIDE - 1, n_cuts)),
             dma((2, SIDE - 1, n_cuts)),
-            dma((2, SIDE - 1, 2)),
-            dma((2, SIDE - 1, 2)),
-            dma((n_chan - 1, 2)),
-            dma((n_chan - 1, 2)),
-            dma((2,)),
+            dma((2, 2, 4)),
+            dma((2, 2, 4)),
+            dma((2, 2)),
+            dma((2, 2)),
+            dma((n_chan - 1, 4)),
+            dma((n_chan - 1, 4)),
+            dma((4,)),
             dma((n_chan - 1,)),
             dma((n_chan - 1,)),
             dma((n_chan - 1,)),
             dma((n_chan - 1,)),
         ],
-        compiler_params=pltpu.CompilerParams(collective_id=0, has_side_effects=True, vmem_limit_bytes=60 * MIB),
+        compiler_params=pltpu.CompilerParams(collective_id=0, has_side_effects=True, vmem_limit_bytes=53 * MIB),
         name="grid_delay",
     )(
         block_tile.reshape(1, -1), tile_owner.reshape(1, -1), tap_offset, cells, weight,
-        jnp.asarray(split_constant().reshape(2, BR, 2 * BR)), vis, jnp.asarray(table_constant(n_chan)), galaxy,
+        vis, jnp.asarray(table_constant(n_chan)), galaxy,
     )
 
 

time: 145 us -> 125 us (0.86)
  Pallas kernels: 139 us -> 117 us
  local copies, waits for them, and re-layouts: 3.14 us -> 5.88 us
    pallas_call x1, Pallas kernels: 139 us -> 117 us  [fused(): pl.pallas_call(functools.partial(kernel, n_chan, cuts), out_shape=(jax.Sh...]
    unnamed x4 -> x10, local copies, waits for them, and re-layouts: 3.14 us -> 5.88 us
where the time goes in v3:
time: 125 us
  Pallas kernels  117 us (94%)
  local copies, waits for them, and re-layouts  5.88 us (5%)
    pallas_call x1, Pallas kernels, fused(): pl.pallas_call(functools.partial(kernel, n_chan, cuts), out_shape=(jax.Sh...  117 us
    unnamed x10, local copies, waits for them, and re-layouts  5.88 us

profile of v3, /device:TPU:1, one launch (start us, length us, event | category | flops | bytes accessed | tf_op | source)
XLA Modules:
  0.0 124.8 jit_solution(17602853654910130839)
XLA Ops:
  0.6 1.0 convert_bitcast_fusion.weight
  1.6 0.0 copy-start
  1.6 0.8 copy-done
  2.4 0.0 copy-start.1
  2.4 0.7 copy-done.1
  3.1 0.0 copy-start.2
  3.1 0.7 copy-done.2
  3.7 0.0 copy-start.3
  3.7 0.7 copy-done.3
  4.4 117.4 %grid_delay.1 = (bf16[19,16,2048]{2,1,0:T(8,128)(2,1)}, f32[19,1024]{1,0:T(8,128)S(1)}) custom-call(s32[1,96]{1,0:T(1,128)S(1)} %bitcast.11, s32[1,160]{1,0:T(1,128)S(1)} %bitcast.10, s32[8]{0:T(128)S(1)} %copy-done.3, s32[96,1,128]{2,1,0:T(1,128)S(1)} %bitcast.9, f32[96,8,128]{2,1,0:T(8,128)S(1)} %convert_bitcast_fusion.weight, ...), custom_call_target="tpu_custom_call" | custom-call | tf_op jit(solution)/shard_map/grid_delay/pallas_call | solution.py:380
  121.7 2.5 %copy.12 = bf16[19,16,2048]{2,1,0:T(8,128)(2,1)} copy(bf16[19,16,2048]{2,1,0:T(8,128)(2,1)} %get-tuple-element.4) | data formatting | bytes 2490368
  124.2 0.6 copy.13
Async XLA Ops:
  1.6 0.8 copy-start
  2.4 0.7 copy-start.1
  3.1 0.7 copy-start.2
  3.7 0.7 copy-start.3

commit v4 on v3

--- a/solution.py
+++ b/solution.py
@@ -104,11 +104,11 @@
 
 def kernel(
     n_chan, cuts,
-    block_tile, tile_owner, tap_offset, cells, weight, vis_hbm, table_hbm, galaxy_hbm,
-    cube, power,
-    vis, wide, table, galaxy, tb, lists, places, lists_sm, places_sm, carry, send, rec0, rec1, rec2, rec3, part, via, got, piece, flat,
-    mine, shares, total_power,
-    load_sem, msend, mrecv, sm_sem, asend, arecv, bsend, brecv, vsend, vrecv, zsend, zrecv, zlocal, psend, precv, gsend, grecv,
+    block_tile, tile_owner, tap_offset, cells, tap_weight, vis_hbm, table_hbm, galaxy_hbm,
+    real, imag, power,
+    vis, wide, weight, table, galaxy, tb, lists, places, lists_sm, places_sm, carry, send, rec0, rec1, rec2, rec3, part, via, got, piece, flat,
+    mine, mine_sent, others,
+    load_sem, msend, mrecv, sm_sem, asend, arecv, bsend, brecv, vsend, vrecv, zsend, zrecv, zlocal, psend, precv,
 ):
     uv, chan = lax.axis_index("uv"), lax.axis_index("chan")
     x, y = uv // SIDE, lax.rem(uv, SIDE)
@@ -153,6 +153,7 @@
     def split(i, _):
         for j in range(4):
             b = 4 * i + j
+            weight[b] = tap_weight[:, pl.ds(pl.multiple_of(b * BR, BR), BR)].astype(F32)
             wide[2 * BR * j : 2 * BR * (j + 1), :] = vis[b].astype(F32)
             for part_of in range(2):
                 rows_of = wide[pl.ds(2 * BR * j + part_of, BR, stride=2), :]
@@ -177,6 +178,7 @@
     for d in range(1, SIDE):
         places_copy(1, d).start()
     carry[...] = jnp.zeros_like(carry)
+    mine_sent[...] = jnp.zeros_like(mine_sent)
     to_scalars.wait()
     loads[0].start()
     loads[1].start()
@@ -309,7 +311,14 @@
     loads[1].wait()
 
     step = 256
-    for lo_s, hi_s in ((0, middle), (middle, SLOTS)):
+    def p_copy(d, i):
+        return pltpu.make_async_remote_copy(
+            mine_sent.at[i], others.at[d - 1, i], psend.at[d - 1, i], precv.at[d - 1, i],
+            device_id=z_peer(d), device_id_type=MESH,
+        )
+
+    parts = ((0, middle), (middle, SLOTS))
+    for i, (lo_s, hi_s) in enumerate(parts):
         for q in range(n_slot_cuts):
             if lo_s <= slot_cuts[q] < hi_s:
                 z_copy(0, q).wait()
@@ -321,37 +330,15 @@
             hi = slice(CH + c * step, CH + (c + 1) * step)
             re = jnp.dot(v, table[:, lo], preferred_element_type=F32).reshape(hi_s - lo_s, rows, step)
             im = jnp.dot(v, table[:, hi], preferred_element_type=F32).reshape(hi_s - lo_s, rows, step)
-            cube[lo_s:hi_s, :, lo] = re.astype(BF16)
-            cube[lo_s:hi_s, :, hi] = im.astype(BF16)
+            real[lo_s:hi_s, :, lo] = re.astype(BF16)
+            imag[lo_s:hi_s, :, lo] = im.astype(BF16)
             product = re * galaxy[lo_s:hi_s, :, lo].astype(F32) + im * galaxy[lo_s:hi_s, :, hi].astype(F32)
-            mine[lo_s:hi_s, lo] = jnp.sum(product, axis=1)
-
-    share = CH // n_chan
-
-    def share_columns(c):
-        return pl.ds(pl.multiple_of(c * share, share), share)
-
-    def p_copy(d):
-        return pltpu.make_async_remote_copy(
-            mine.at[:, share_columns(lax.rem(chan + d, n_chan))], shares.at[d - 1], psend.at[d - 1], precv.at[d - 1],
-            device_id=z_peer(d), device_id_type=MESH,
-        )
-
-    def g_copy(d):
-        own = total_power.at[:, share_columns(chan)]
-        return pltpu.make_async_remote_copy(
-            own, own, gsend.at[d - 1], grecv.at[d - 1], device_id=z_peer(d), device_id_type=MESH
-        )
-
-    for d in range(1, n_chan):
-        p_copy(d).start()
-    total = mine[:, share_columns(chan)]
-    for d in range(1, n_chan):
-        p_copy(d).wait_recv()
-        total = total + shares[d - 1]
-    total_power[:, share_columns(chan)] = total / F32(math.sqrt(TC))
-    for d in range(1, n_chan):
-        g_copy(d).start()
+            sums = jnp.sum(product, axis=1)
+            mine[lo_s:hi_s, lo] = sums
+            mine_sent[i, 0 : hi_s - lo_s, lo] = sums.astype(BF16)
+        for d in range(1, n_chan):
+            p_copy(d, i).start()
+
     for h in range(2):
         for g in range(1, SIDE):
             for k in range(n_cuts):
@@ -363,10 +350,14 @@
     for d in range(1, n_chan):
         for q in range(n_slot_cuts):
             z_copy(d, q).wait_send()
-        p_copy(d).wait_send()
-    for d in range(1, n_chan):
-        g_copy(d).wait()
-    power[...] = total_power[...]
+        for i in range(2):
+            p_copy(d, i).wait_send()
+    for i, (lo_s, hi_s) in enumerate(parts):
+        total = mine[lo_s:hi_s, :]
+        for d in range(1, n_chan):
+            p_copy(d, i).wait_recv()
+            total = total + others[d - 1, i, 0 : hi_s - lo_s, :].astype(F32)
+        power[lo_s:hi_s, :] = total
 
 
 def fused(n_chan, cuts, block_tile, tile_owner, tap_offset, cells, weight, vis, galaxy):
@@ -380,14 +371,16 @@
     return pl.pallas_call(
         functools.partial(kernel, n_chan, cuts),
         out_shape=(
-            jax.ShapeDtypeStruct((SLOTS, rows, 2 * CH), BF16),
+            jax.ShapeDtypeStruct((SLOTS, rows, CH), BF16),
+            jax.ShapeDtypeStruct((SLOTS, rows, CH), BF16),
             jax.ShapeDtypeStruct((SLOTS, CH), F32),
         ),
         in_specs=[vmem, vmem, smem, vmem, vmem, hbm, hbm, hbm],
-        out_specs=(vmem, vmem),
+        out_specs=(vmem, vmem, vmem),
         scratch_shapes=[
             pltpu.VMEM(vis.shape, BF16),
             pltpu.VMEM((4 * 2 * BR, width), F32),
+            pltpu.VMEM((nb, KT, BR), F32),
             pltpu.VMEM((2 * CH, 2 * CH), BF16),
             pltpu.VMEM(galaxy.shape, BF16),
             pltpu.VMEM((8, 256), jnp.int32),
@@ -404,8 +397,8 @@
             pltpu.VMEM((n_chan, SLOTS, rows, 2 * width), BF16),
             pltpu.VMEM((SLOTS, rows, 2 * CH), BF16),
             pltpu.VMEM((SLOTS, CH), F32),
-            pltpu.VMEM((n_chan - 1, SLOTS, CH // n_chan), F32),
-            pltpu.VMEM((SLOTS, CH), F32),
+            pltpu.VMEM((2, 16, CH), BF16),
+            pltpu.VMEM((n_chan - 1, 2, 16, CH), BF16),
             dma((6,)),
             dma((2 * SIDE,)),
             dma((2 * SIDE,)),
@@ -419,12 +412,10 @@
             dma((n_chan - 1, 4)),
             dma((n_chan - 1, 4)),
             dma((4,)),
-            dma((n_chan - 1,)),
-            dma((n_chan - 1,)),
-            dma((n_chan - 1,)),
-            dma((n_chan - 1,)),
+            dma((n_chan - 1, 2)),
+            dma((n_chan - 1, 2)),
         ],
-        compiler_params=pltpu.CompilerParams(collective_id=0, has_side_effects=True, vmem_limit_bytes=53 * MIB),
+        compiler_params=pltpu.CompilerParams(collective_id=0, has_side_effects=True, vmem_limit_bytes=60 * MIB),
         name="grid_delay",
     )(
         block_tile.reshape(1, -1), tile_owner.reshape(1, -1), tap_offset, cells, weight,
@@ -439,10 +430,10 @@
         nb = block_tile.shape[0]
         blocks = vis.reshape(nb, 2 * BR, vis.shape[2])
         cells = row_cell.reshape(nb, 1, BR)
-        weight = jnp.transpose(tap_weight.reshape(KT, nb, BR), (1, 0, 2)).astype(F32)
-        return fused(
-            n_chan, (0, 3, 11, 22, 33, 44), block_tile, tile_owner, tap_offset, cells, weight, blocks, galaxy
-        )
+        real, imag, power = fused(
+            n_chan, (0, 1, 4, 11, 22, 33, 44), block_tile, tile_owner, tap_offset, cells, tap_weight, blocks, galaxy
+        )
+        return jnp.concatenate([real, imag], axis=-1), power / F32(math.sqrt(TC))
 
     return jax.shard_map(
         body,

time: 125 us -> 120 us (0.960)
  local copies, waits for them, and re-layouts: 5.88 us -> 0.01 us
  other arithmetic: 0.95 us -> 3.1 us
    unnamed x10 -> x2, local copies, waits for them, and re-layouts: 5.88 us -> 0.01 us
    concatenate x0 -> x1, other arithmetic: none -> 2.45 us  [body(): return (jnp.concatenate([real, imag], axis=-1), power / F32(math.sqrt(TC)))]
where the time goes in v4:
time: 120 us
  Pallas kernels  116 us (97%)
  other arithmetic  3.1 us (3%)
    pallas_call x1, Pallas kernels, fused(): pl.pallas_call(functools.partial(kernel, n_chan, cuts), out_shape=(jax.Sh...  116 us
    concatenate x1, other arithmetic, body(): return (jnp.concatenate([real, imag], axis=-1), power / F32(math.sqrt(TC)))  2.45 us

profile of v4, /device:TPU:1, one launch (start us, length us, event | category | flops | bytes accessed | tf_op | source)
XLA Modules:
  0.0 120.1 jit_solution(2472084279519327711)
XLA Ops:
  0.6 116.4 %grid_delay.1 = (bf16[19,16,1024]{2,1,0:T(8,128)(2,1)}, bf16[19,16,1024]{2,1,0:T(8,128)(2,1)}, f32[19,1024]{1,0:T(8,128)}) custom-call(s32[1,96]{1,0:T(1,128)} %bitcast.7, s32[1,160]{1,0:T(1,128)} %bitcast.6, s32[8]{0:T(128)} %tap_offset.1, s32[96,1,128]{2,1,0:T(1,128)} %bitcast.5, bf16[8,12288]{1,0:T(8,128)(2,1)} %tap_weight.1, ...), custom_call_target="tpu_custom_call" | custom-call | tf_op jit(solution)/shard_map/grid_delay/pallas_call | solution.py:371
  117.0 0.0 copy-start
  117.0 2.4 %pad_maximum_fusion = bf16[19,16,2048]{2,1,0:T(8,128)(2,1)} fusion(bf16[19,16,1024]{2,1,0:T(8,128)(2,1)} %get-tuple-element.6, bf16[19,16,1024]{2,1,0:T(8,128)(2,1)} %get-tuple-element.5), kind=kLoop, calls=%fused_computation | loop fusion | flops 2490368 | bytes 2490368 | tf_op jit(solution)/shard_map/concatenate | solution.py:436
  119.5 0.0 copy-done
  119.5 0.7 broadcast_multiply_fusion
Async XLA Ops:
  117.0 2.5 %copy-start = (f32[19,1024]{1,0:T(8,128)S(1)}, f32[19,1024]{1,0:T(8,128)}, u32[]{:S(2)}) copy-start(f32[19,1024]{1,0:T(8,128)} %get-tuple-element.7) | copy-start | bytes 233476

commit v5 on v4

--- a/solution.py
+++ b/solution.py
@@ -107,7 +107,7 @@
     block_tile, tile_owner, tap_offset, cells, tap_weight, vis_hbm, table_hbm, galaxy_hbm,
     real, imag, power,
     vis, wide, weight, table, galaxy, tb, lists, places, lists_sm, places_sm, carry, send, rec0, rec1, rec2, rec3, part, via, got, piece, flat,
-    mine, mine_sent, others,
+    mine, mine_sent, others, last_sent, last_others,
     load_sem, msend, mrecv, sm_sem, asend, arecv, bsend, brecv, vsend, vrecv, zsend, zrecv, zlocal, psend, precv,
 ):
     uv, chan = lax.axis_index("uv"), lax.axis_index("chan")
@@ -313,11 +313,11 @@
     step = 256
     def p_copy(d, i):
         return pltpu.make_async_remote_copy(
-            mine_sent.at[i], others.at[d - 1, i], psend.at[d - 1, i], precv.at[d - 1, i],
+            (mine_sent, last_sent)[i], (others, last_others)[i].at[d - 1], psend.at[d - 1, i], precv.at[d - 1, i],
             device_id=z_peer(d), device_id_type=MESH,
         )
 
-    parts = ((0, middle), (middle, SLOTS))
+    parts = ((0, slot_cuts[-2]), (slot_cuts[-2], SLOTS))
     for i, (lo_s, hi_s) in enumerate(parts):
         for q in range(n_slot_cuts):
             if lo_s <= slot_cuts[q] < hi_s:
@@ -335,7 +335,10 @@
             product = re * galaxy[lo_s:hi_s, :, lo].astype(F32) + im * galaxy[lo_s:hi_s, :, hi].astype(F32)
             sums = jnp.sum(product, axis=1)
             mine[lo_s:hi_s, lo] = sums
-            mine_sent[i, 0 : hi_s - lo_s, lo] = sums.astype(BF16)
+            if i == 0:
+                mine_sent[0 : hi_s - lo_s, lo] = sums.astype(BF16)
+            else:
+                last_sent[4 * c : 4 * c + 4, :] = sums.astype(BF16)
         for d in range(1, n_chan):
             p_copy(d, i).start()
 
@@ -352,12 +355,20 @@
             z_copy(d, q).wait_send()
         for i in range(2):
             p_copy(d, i).wait_send()
-    for i, (lo_s, hi_s) in enumerate(parts):
-        total = mine[lo_s:hi_s, :]
+    first = slot_cuts[-2]
+    total = mine[:first, :]
+    for d in range(1, n_chan):
+        p_copy(d, 0).wait_recv()
+        total = total + others[d - 1, :first, :].astype(F32)
+    power[:first, :] = total / F32(math.sqrt(TC))
+    for d in range(1, n_chan):
+        p_copy(d, 1).wait_recv()
+    for c in range(CH // step):
+        columns = slice(c * step, (c + 1) * step)
+        total = mine[first:, columns]
         for d in range(1, n_chan):
-            p_copy(d, i).wait_recv()
-            total = total + others[d - 1, i, 0 : hi_s - lo_s, :].astype(F32)
-        power[lo_s:hi_s, :] = total
+            total = total + last_others[d - 1, 4 * c : 4 * c + 4, :].astype(F32)
+        power[first:, columns] = total / F32(math.sqrt(TC))
 
 
 def fused(n_chan, cuts, block_tile, tile_owner, tap_offset, cells, weight, vis, galaxy):
@@ -397,8 +408,10 @@
             pltpu.VMEM((n_chan, SLOTS, rows, 2 * width), BF16),
             pltpu.VMEM((SLOTS, rows, 2 * CH), BF16),
             pltpu.VMEM((SLOTS, CH), F32),
-            pltpu.VMEM((2, 16, CH), BF16),
-            pltpu.VMEM((n_chan - 1, 2, 16, CH), BF16),
+            pltpu.VMEM((16, CH), BF16),
+            pltpu.VMEM((n_chan - 1, 16, CH), BF16),
+            pltpu.VMEM((16, CH // 4), BF16),
+            pltpu.VMEM((n_chan - 1, 16, CH // 4), BF16),
             dma((6,)),
             dma((2 * SIDE,)),
             dma((2 * SIDE,)),
@@ -423,6 +436,33 @@
     )
 
 
+def outputs_kernel(real, imag, power, cube, power_out, sem):
+    copies = [
+        pltpu.make_async_copy(real, cube.at[:, :, pl.ds(0, CH)], sem.at[0]),
+        pltpu.make_async_copy(imag, cube.at[:, :, pl.ds(CH, CH)], sem.at[1]),
+        pltpu.make_async_copy(power, power_out, sem.at[2]),
+    ]
+    for copy in copies:
+        copy.start()
+    for copy in copies:
+        copy.wait()
+
+
+def outputs(real, imag, power):
+    hbm = pl.BlockSpec(memory_space=pl.ANY)
+    return pl.pallas_call(
+        outputs_kernel,
+        out_shape=(
+            jax.ShapeDtypeStruct((*real.shape[:2], 2 * CH), BF16),
+            jax.ShapeDtypeStruct(power.shape, F32),
+        ),
+        in_specs=[pl.BlockSpec(memory_space=pltpu.VMEM)] * 3,
+        out_specs=(hbm, hbm),
+        scratch_shapes=[pltpu.SemaphoreType.DMA((3,))],
+        name="outputs",
+    )(real, imag, power)
+
+
 def solution(mesh):
     n_chan = mesh.shape["chan"]
 
@@ -433,7 +473,7 @@
         real, imag, power = fused(
             n_chan, (0, 1, 4, 11, 22, 33, 44), block_tile, tile_owner, tap_offset, cells, tap_weight, blocks, galaxy
         )
-        return jnp.concatenate([real, imag], axis=-1), power / F32(math.sqrt(TC))
+        return outputs(real, imag, power)
 
     return jax.shard_map(
         body,

time: 120 us -> 118 us (0.983)
  other arithmetic: 3.1 us -> 0 us
    concatenate x1 -> x0, other arithmetic: 2.45 us -> none  [body(): return (jnp.concatenate([real, imag], axis=-1), power / F32(math.sqrt(TC)))]
    pallas_call x0 -> x1, Pallas kernels: none -> 2.34 us  [outputs(): pl.pallas_call(outputs_kernel, out_shape=(jax.ShapeDtypeStruct((*real.sha...]
    pallas_call x1, Pallas kernels: 116 us -> 115 us  [fused(): pl.pallas_call(functools.partial(kernel, n_chan, cuts), out_shape=(jax.Sh...]
where the time goes in v5:
time: 118 us
  Pallas kernels  117 us (99%)
    pallas_call x1, Pallas kernels, fused(): pl.pallas_call(functools.partial(kernel, n_chan, cuts), out_shape=(jax.Sh...  115 us

profile of v5, /device:TPU:1, one launch (start us, length us, event | category | flops | bytes accessed | tf_op | source)
XLA Modules:
  0.0 118.0 jit_solution(9420414091987655331)
XLA Ops:
  0.6 115.0 %grid_delay.1 = (bf16[19,16,1024]{2,1,0:T(8,128)(2,1)}, bf16[19,16,1024]{2,1,0:T(8,128)(2,1)}, f32[19,1024]{1,0:T(8,128)}) custom-call(s32[1,96]{1,0:T(1,128)} %bitcast.7, s32[1,160]{1,0:T(1,128)} %bitcast.6, s32[8]{0:T(128)} %tap_offset.1, s32[96,1,128]{2,1,0:T(1,128)} %bitcast.5, bf16[8,12288]{1,0:T(8,128)(2,1)} %tap_weight.1, ...), custom_call_target="tpu_custom_call" | custom-call | tf_op jit(solution)/shard_map/grid_delay/pallas_call | solution.py:382
  115.7 2.3 %outputs.1 = (bf16[19,16,2048]{2,1,0:T(8,128)(2,1)}, f32[19,1024]{1,0:T(8,128)}) custom-call(bf16[19,16,1024]{2,1,0:T(8,128)(2,1)} %get-tuple-element.5.real, bf16[19,16,1024]{2,1,0:T(8,128)(2,1)} %get-tuple-element.6.imag, f32[19,1024]{1,0:T(8,128)} %get-tuple-element.7.power), custom_call_target="tpu_custom_call" | custom-call | tf_op jit(solution)/shard_map/outputs/pallas_call | solution.py:453

commit v6 on v5

--- a/solution.py
+++ b/solution.py
@@ -436,16 +436,24 @@
     )
 
 
-def outputs_kernel(real, imag, power, cube, power_out, sem):
-    copies = [
-        pltpu.make_async_copy(real, cube.at[:, :, pl.ds(0, CH)], sem.at[0]),
-        pltpu.make_async_copy(imag, cube.at[:, :, pl.ds(CH, CH)], sem.at[1]),
-        pltpu.make_async_copy(power, power_out, sem.at[2]),
-    ]
-    for copy in copies:
-        copy.start()
-    for copy in copies:
-        copy.wait()
+def outputs_kernel(real, imag, power, cube, power_out, held, held_power, sem):
+    loads, stores = [], []
+    cuts = (0, 5, 10, 15, SLOTS)
+    for k, half in enumerate((real, imag)):
+        for i in range(4):
+            cut = pl.ds(cuts[i], cuts[i + 1] - cuts[i])
+            n = len(loads)
+            loads.append(pltpu.make_async_copy(half.at[cut], held.at[k, cut], sem.at[0, n]))
+            stores.append(pltpu.make_async_copy(held.at[k, cut], cube.at[cut, :, pl.ds(k * CH, CH)], sem.at[1, n]))
+    loads.append(pltpu.make_async_copy(power, held_power, sem.at[0, 8]))
+    stores.append(pltpu.make_async_copy(held_power, power_out, sem.at[1, 8]))
+    for load in loads:
+        load.start()
+    for load, store in zip(loads, stores):
+        load.wait()
+        store.start()
+    for store in stores:
+        store.wait()
 
 
 def outputs(real, imag, power):
@@ -456,9 +464,13 @@
             jax.ShapeDtypeStruct((*real.shape[:2], 2 * CH), BF16),
             jax.ShapeDtypeStruct(power.shape, F32),
         ),
-        in_specs=[pl.BlockSpec(memory_space=pltpu.VMEM)] * 3,
+        in_specs=[hbm] * 3,
         out_specs=(hbm, hbm),
-        scratch_shapes=[pltpu.SemaphoreType.DMA((3,))],
+        scratch_shapes=[
+            pltpu.VMEM((2, *real.shape), BF16),
+            pltpu.VMEM(power.shape, F32),
+            pltpu.SemaphoreType.DMA((2, 9)),
+        ],
         name="outputs",
     )(real, imag, power)
 

time: 118 us -> 118 us (level)
  no operation moved by 1% of the time
where the time goes in v6:
time: 118 us
  Pallas kernels  117 us (99%)
    pallas_call x1, Pallas kernels, fused(): pl.pallas_call(functools.partial(kernel, n_chan, cuts), out_shape=(jax.Sh...  115 us

profile of v6, /device:TPU:1, one launch (start us, length us, event | category | flops | bytes accessed | tf_op | source)
XLA Modules:
  0.0 117.9 jit_solution(5509280474061567873)
XLA Ops:
  0.6 115.0 %grid_delay.1 = (bf16[19,16,1024]{2,1,0:T(8,128)(2,1)}, bf16[19,16,1024]{2,1,0:T(8,128)(2,1)}, f32[19,1024]{1,0:T(8,128)}) custom-call(s32[1,96]{1,0:T(1,128)} %bitcast.7, s32[1,160]{1,0:T(1,128)} %bitcast.6, s32[8]{0:T(128)} %tap_offset.1, s32[96,1,128]{2,1,0:T(1,128)} %bitcast.5, bf16[8,12288]{1,0:T(8,128)(2,1)} %tap_weight.1, ...), custom_call_target="tpu_custom_call" | custom-call | tf_op jit(solution)/shard_map/grid_delay/pallas_call | solution.py:382
  115.7 2.2 %outputs.1 = (bf16[19,16,2048]{2,1,0:T(8,128)(2,1)}, f32[19,1024]{1,0:T(8,128)}) custom-call(bf16[19,16,1024]{2,1,0:T(8,128)(2,1)} %get-tuple-element.5.real, bf16[19,16,1024]{2,1,0:T(8,128)(2,1)} %get-tuple-element.6.imag, f32[19,1024]{1,0:T(8,128)} %get-tuple-element.7.power), custom_call_target="tpu_custom_call" | custom-call | tf_op jit(solution)/shard_map/outputs/pallas_call | solution.py:461
